TPU v7x, 512 devices: a whole 4x8x8 slice. The times are simulated.
512 devices in a mesh: seq: 64 (over y, z), head: 8 (over x, core).
Axes of the slice: x: 4, y: 8, z: 8, core: 2. Of those that a mesh axis runs over, the one named last changes fastest.
Arguments:
- queries: bfloat16 [32768, 4096], P('seq', 'head'), may hold values from -100 to 100
- key_rows: bfloat16 [32768, 1024], P('seq', 'head'), may hold values from -6.1 to 6.1
- value_rows: bfloat16 [32768, 1024], P('seq', 'head'), may hold values from -6 to 6
- doc_blocks: int32 [32], replicated, may hold values from 1 to 32, 256 in all
Outputs:
- attended: bfloat16 [32768, 4096], P(('seq', 'head'))
Inputs may be any that keep to these rules, and one draw needn't show every extreme that they name: `doc_blocks`: lengths in blocks of 128 tokens, in order along the sequence; they sum to 256 and the longest is exactly 32.
All inputs are finite; a program needn't handle non-finite values.
Results may differ from a plain program's by a relative error of at most 0.005.
Values may be sent and summed in bfloat16 or wider, within the bound.
A program may use at most 64 MiB of HBM per device.

v0:
```python
import math

import jax
import jax.numpy as jnp
from jax import lax
from jax.sharding import PartitionSpec as P

QH = 32
KVH = 8
HD = 128
B = 128
HOPS = 8


masked_score = -1e30


def shifted(block, axis, distance):
    devices = range(lax.axis_size(axis))
    route = [(i - distance, i) for i in devices if i - distance in devices]
    return lax.ppermute(block, axis, route)


def doc_index(positions, doc_ends):
    block_index = jnp.floor_divide(positions, B)
    return jnp.sum((block_index[:, None] >= doc_ends[None, :]).astype(jnp.int32), axis=1)


def body(queries, key_rows, value_rows, doc_blocks):
    tok_rows = queries.shape[0]
    kv_heads = key_rows.shape[1] // HD
    group_size = QH // KVH
    score_scale = 1.0 / math.sqrt(HD)
    device_index = lax.axis_index("seq")
    doc_ends = jnp.cumsum(doc_blocks)
    first_pos = device_index * tok_rows
    query_pos = first_pos + jnp.arange(tok_rows, dtype=jnp.int32)
    query_doc = doc_index(query_pos, doc_ends)
    query_mat = queries.reshape(tok_rows, kv_heads, group_size, HD)

    def attend(state_in, kv_pair, key_start):
        row_max, row_total, weighted = state_in
        count_keys = kv_pair.shape[1]
        key_pos = key_start + jnp.arange(count_keys, dtype=jnp.int32)
        key_doc = doc_index(key_pos, doc_ends)
        visible = (
            (key_doc[None, :] == query_doc[:, None])
            & (key_pos[None, :] <= query_pos[:, None])
            & (key_pos[None, :] >= 0)
        )
        key_mat = kv_pair[0].reshape(count_keys, kv_heads, HD)
        value_mat = kv_pair[1].reshape(count_keys, kv_heads, HD)
        scores = (
            jnp.einsum("qhgd,khd->hgqk", query_mat, key_mat, preferred_element_type=jnp.float32)
            * score_scale
        )
        scores = jnp.where(visible, scores, masked_score)
        new_max = jnp.maximum(row_max, jnp.max(scores, axis=-1))
        weights = jnp.where(visible, jnp.exp(scores - new_max[..., None]), 0.0)
        shrink = jnp.exp(row_max - new_max)
        row_total = row_total * shrink + jnp.sum(weights, axis=-1)
        weighted = weighted * shrink[..., None] + jnp.einsum(
            "hgqk,khd->hgqd",
            weights.astype(jnp.bfloat16),
            value_mat,
            preferred_element_type=jnp.float32,
        )
        return (new_max, row_total, weighted)

    def visit_piece(state_in, kv_pair, key_start):
        return attend(state_in, kv_pair, key_start)

    state = (
        jnp.full((kv_heads, group_size, tok_rows), masked_score, jnp.float32),
        jnp.zeros((kv_heads, group_size, tok_rows), jnp.float32),
        jnp.zeros((kv_heads, group_size, tok_rows, HD), jnp.float32),
    )
    own_pair = jnp.stack([key_rows, value_rows])
    state = visit_piece(state, own_pair, first_pos)

    def one_turn(step, carried):
        kv_pair, state_in = carried
        kv_pair = shifted(kv_pair, "seq", 1)
        return (kv_pair, visit_piece(state_in, kv_pair, first_pos - step * tok_rows))

    _, state = lax.fori_loop(1, HOPS + 1, one_turn, (own_pair, state))
    row_max, row_total, weighted = state
    result = weighted / row_total[..., None]
    outputs = (
        jnp.transpose(result, (2, 0, 1, 3))
        .reshape(tok_rows, kv_heads * group_size * HD)
        .astype(jnp.bfloat16)
    )
    return lax.all_to_all(outputs, "head", split_axis=0, concat_axis=1, tiled=True)


def solution(mesh):
    in_specs = (P("seq", "head"), P("seq", "head"), P("seq", "head"), P())
    out_specs = P(("seq", "head"), None)
    return jax.shard_map(body, mesh=mesh, in_specs=in_specs, out_specs=out_specs, check_vma=False)
```

profile of v0, /device:TPU:32, one launch (start us, length us, event | category | flops | bytes accessed | tf_op | source)
XLA Modules:
  0.0 157.9 jit_solution(5178187514613865740)
XLA Ops:
  0.9 1.3 copy.28
  2.6 2.0 %fusion.25 = (f32[4,512]{1,0:T(4,128)S(1)}, f32[512,512,4]{1,0,2:T(8,128)S(1)}) fusion(pred[512,512]{0,1:T(8,128)(4,1)S(1)} %and_and_fusion.1, bf16[512,128]{1,0:T(8,128)(2,1)} %param.7, bf16[512,512]{1,0:T(8,128)(2,1)} %param.6), kind=kOutput, calls=%fused_computation.37 | convolution fusion | flops 271579136 | bytes 5120000 | tf_op jit(solution)/shard_map/qhgd,khd->hgqk/dot_general | solution.py:54
  4.7 1.0 fusion.27
  5.7 0.8 copy-done
  6.9 3.7 %fusion.35 = f32[1,4,512,128]{3,2,1,0:T(8,128)S(1)} fusion(f32[512,512,4]{1,0,2:T(8,128)} %copy-done, f32[4,512]{1,0:T(4,128)S(1)} %get-tuple-element.349, pred[512,512]{0,1:T(8,128)(4,1)S(1)} %and_and_fusion.1, f32[4,512]{1,0:T(4,128)S(1)} %get-tuple-element.347, bf16[512,128]{1,0:T(8,128)(2,1)S(1)} %copy-done.2), kind=kOutput, calls=%fused_computation.44 | convolution fusion | flops 273940480 | bytes 5652480 | tf_op jit(solution)/shard_map/hgqk,khd->hgqd/dot_general | solution.py:62
  10.6 131.0 %while.23 = (s32[]{:T(128)}, bf16[2,512,128]{2,1,0:T(8,128)(2,1)S(1)}, f32[1,4,512]{2,1,0:T(4,128)S(1)}, f32[1,4,512]{2,1,0:T(4,128)S(1)}, f32[1,4,512,128]{3,2,...) while((s32[]{:T(128)}, ...), condition=%wide.region_8.9_spmd.clone.clone, body=%wide.region_4.8_spmd.clone.clone.sunk | while | flops 552140288 | bytes 18238780 | solution.py:86
  10.6 4.3 %collective-permute-start = (bf16[2,512,128]{2,1,0:T(8,128)(2,1)S(1)}, bf16[2,512,128]{2,1,0:T(8,128)(2,1)S(1)}, u32[]{:S(2)}, u32[]{:S(2)}) collective-permute-start(bf16[2,512,128]{2,1,0:T(8,128)(2,1)S(1)} %get-tuple-element.433), channel_id=1, source_target_pairs={{0,8},{8,16},{16,24},{24,32},{32,40},{40,48},{48,56},{56,64},{64,7... | collective-permute-start | bytes 786440 | tf_op jit(solution)/shard_map/while/body/eval_jaxpr/ppermute | solution.py:21
  15.3 12.4 %collective-permute-done = bf16[2,512,128]{2,1,0:T(8,128)(2,1)S(1)} collective-permute-done((bf16[2,512,128]{2,1,0:T(8,128)(2,1)S(1)}, bf16[2,512,128]{2,1,0:T(8,128)(2,1)S(1)}, u32[]{:S(2)}, u32[]{:S(2)}) %collective-permute-start) | collective-permute-done | bytes 262176 | tf_op jit(solution)/shard_map/while/body/eval_jaxpr/ppermute | solution.py:21
  27.7 0.9 fusion.61
  28.6 1.0 fusion.63
  29.7 1.9 %fusion.64 = f32[1,4,512,128]{3,2,1,0:T(8,128)S(1)} fusion(f32[512,512,4]{1,0,2:T(8,128)S(1)} %get-tuple-element.419, f32[4,512]{1,0:T(4,128)S(1)} %bitcast.138, pred[512,512]{0,1:T(8,128)(4,1)S(1)} %and_and_fusion.3, f32[1,4,512,128]{3,2,1,0:T(8,128)S(1)} %get-tuple-element.436, f32[4,512]{1,0:T(4,128)S(1)} %get-tuple-element.420, ...), kind=kOutput, calls=%fused_computation.10.clone.1 | convolution fusion | flops 274202624 | bytes 6701056 | tf_op jit(solution)/shard_map/while/body/eval_jaxpr/hgqk,khd->hgqd/dot_general | solution.py:62
  31.7 1.9 %collective-permute-start = (bf16[2,512,128]{2,1,0:T(8,128)(2,1)S(1)}, bf16[2,512,128]{2,1,0:T(8,128)(2,1)S(1)}, u32[]{:S(2)}, u32[]{:S(2)}) collective-permute-start(bf16[2,512,128]{2,1,0:T(8,128)(2,1)S(1)} %get-tuple-element.433), channel_id=1, source_target_pairs={{0,8},{8,16},{16,24},{24,32},{32,40},{40,48},{48,56},{56,64},{64,7... | collective-permute-start | bytes 786440 | tf_op jit(solution)/shard_map/while/body/eval_jaxpr/ppermute | solution.py:21
  34.1 10.3 %collective-permute-done = bf16[2,512,128]{2,1,0:T(8,128)(2,1)S(1)} collective-permute-done((bf16[2,512,128]{2,1,0:T(8,128)(2,1)S(1)}, bf16[2,512,128]{2,1,0:T(8,128)(2,1)S(1)}, u32[]{:S(2)}, u32[]{:S(2)}) %collective-permute-start) | collective-permute-done | bytes 262176 | tf_op jit(solution)/shard_map/while/body/eval_jaxpr/ppermute | solution.py:21
  44.4 0.9 fusion.61
  45.3 1.0 fusion.63
  46.4 1.9 %fusion.64 = f32[1,4,512,128]{3,2,1,0:T(8,128)S(1)} fusion(f32[512,512,4]{1,0,2:T(8,128)S(1)} %get-tuple-element.419, f32[4,512]{1,0:T(4,128)S(1)} %bitcast.138, pred[512,512]{0,1:T(8,128)(4,1)S(1)} %and_and_fusion.3, f32[1,4,512,128]{3,2,1,0:T(8,128)S(1)} %get-tuple-element.436, f32[4,512]{1,0:T(4,128)S(1)} %get-tuple-element.420, ...), kind=kOutput, calls=%fused_computation.10.clone.1 | convolution fusion | flops 274202624 | bytes 6701056 | tf_op jit(solution)/shard_map/while/body/eval_jaxpr/hgqk,khd->hgqd/dot_general | solution.py:62
  48.3 1.9 %collective-permute-start = (bf16[2,512,128]{2,1,0:T(8,128)(2,1)S(1)}, bf16[2,512,128]{2,1,0:T(8,128)(2,1)S(1)}, u32[]{:S(2)}, u32[]{:S(2)}) collective-permute-start(bf16[2,512,128]{2,1,0:T(8,128)(2,1)S(1)} %get-tuple-element.433), channel_id=1, source_target_pairs={{0,8},{8,16},{16,24},{24,32},{32,40},{40,48},{48,56},{56,64},{64,7... | collective-permute-start | bytes 786440 | tf_op jit(solution)/shard_map/while/body/eval_jaxpr/ppermute | solution.py:21
  50.7 9.4 %collective-permute-done = bf16[2,512,128]{2,1,0:T(8,128)(2,1)S(1)} collective-permute-done((bf16[2,512,128]{2,1,0:T(8,128)(2,1)S(1)}, bf16[2,512,128]{2,1,0:T(8,128)(2,1)S(1)}, u32[]{:S(2)}, u32[]{:S(2)}) %collective-permute-start) | collective-permute-done | bytes 262176 | tf_op jit(solution)/shard_map/while/body/eval_jaxpr/ppermute | solution.py:21
  60.1 0.9 fusion.61
  61.0 1.0 fusion.63
  62.1 1.9 %fusion.64 = f32[1,4,512,128]{3,2,1,0:T(8,128)S(1)} fusion(f32[512,512,4]{1,0,2:T(8,128)S(1)} %get-tuple-element.419, f32[4,512]{1,0:T(4,128)S(1)} %bitcast.138, pred[512,512]{0,1:T(8,128)(4,1)S(1)} %and_and_fusion.3, f32[1,4,512,128]{3,2,1,0:T(8,128)S(1)} %get-tuple-element.436, f32[4,512]{1,0:T(4,128)S(1)} %get-tuple-element.420, ...), kind=kOutput, calls=%fused_computation.10.clone.1 | convolution fusion | flops 274202624 | bytes 6701056 | tf_op jit(solution)/shard_map/while/body/eval_jaxpr/hgqk,khd->hgqd/dot_general | solution.py:62
  64.0 1.9 %collective-permute-start = (bf16[2,512,128]{2,1,0:T(8,128)(2,1)S(1)}, bf16[2,512,128]{2,1,0:T(8,128)(2,1)S(1)}, u32[]{:S(2)}, u32[]{:S(2)}) collective-permute-start(bf16[2,512,128]{2,1,0:T(8,128)(2,1)S(1)} %get-tuple-element.433), channel_id=1, source_target_pairs={{0,8},{8,16},{16,24},{24,32},{32,40},{40,48},{48,56},{56,64},{64,7... | collective-permute-start | bytes 786440 | tf_op jit(solution)/shard_map/while/body/eval_jaxpr/ppermute | solution.py:21
  66.4 9.2 %collective-permute-done = bf16[2,512,128]{2,1,0:T(8,128)(2,1)S(1)} collective-permute-done((bf16[2,512,128]{2,1,0:T(8,128)(2,1)S(1)}, bf16[2,512,128]{2,1,0:T(8,128)(2,1)S(1)}, u32[]{:S(2)}, u32[]{:S(2)}) %collective-permute-start) | collective-permute-done | bytes 262176 | tf_op jit(solution)/shard_map/while/body/eval_jaxpr/ppermute | solution.py:21
  75.6 0.9 fusion.61
  76.5 1.0 fusion.63
  77.6 1.9 %fusion.64 = f32[1,4,512,128]{3,2,1,0:T(8,128)S(1)} fusion(f32[512,512,4]{1,0,2:T(8,128)S(1)} %get-tuple-element.419, f32[4,512]{1,0:T(4,128)S(1)} %bitcast.138, pred[512,512]{0,1:T(8,128)(4,1)S(1)} %and_and_fusion.3, f32[1,4,512,128]{3,2,1,0:T(8,128)S(1)} %get-tuple-element.436, f32[4,512]{1,0:T(4,128)S(1)} %get-tuple-element.420, ...), kind=kOutput, calls=%fused_computation.10.clone.1 | convolution fusion | flops 274202624 | bytes 6701056 | tf_op jit(solution)/shard_map/while/body/eval_jaxpr/hgqk,khd->hgqd/dot_general | solution.py:62
  79.5 1.9 %collective-permute-start = (bf16[2,512,128]{2,1,0:T(8,128)(2,1)S(1)}, bf16[2,512,128]{2,1,0:T(8,128)(2,1)S(1)}, u32[]{:S(2)}, u32[]{:S(2)}) collective-permute-start(bf16[2,512,128]{2,1,0:T(8,128)(2,1)S(1)} %get-tuple-element.433), channel_id=1, source_target_pairs={{0,8},{8,16},{16,24},{24,32},{32,40},{40,48},{48,56},{56,64},{64,7... | collective-permute-start | bytes 786440 | tf_op jit(solution)/shard_map/while/body/eval_jaxpr/ppermute | solution.py:21
  81.9 9.2 %collective-permute-done = bf16[2,512,128]{2,1,0:T(8,128)(2,1)S(1)} collective-permute-done((bf16[2,512,128]{2,1,0:T(8,128)(2,1)S(1)}, bf16[2,512,128]{2,1,0:T(8,128)(2,1)S(1)}, u32[]{:S(2)}, u32[]{:S(2)}) %collective-permute-start) | collective-permute-done | bytes 262176 | tf_op jit(solution)/shard_map/while/body/eval_jaxpr/ppermute | solution.py:21
  91.1 0.9 fusion.61
  92.0 1.0 fusion.63
  93.1 1.9 %fusion.64 = f32[1,4,512,128]{3,2,1,0:T(8,128)S(1)} fusion(f32[512,512,4]{1,0,2:T(8,128)S(1)} %get-tuple-element.419, f32[4,512]{1,0:T(4,128)S(1)} %bitcast.138, pred[512,512]{0,1:T(8,128)(4,1)S(1)} %and_and_fusion.3, f32[1,4,512,128]{3,2,1,0:T(8,128)S(1)} %get-tuple-element.436, f32[4,512]{1,0:T(4,128)S(1)} %get-tuple-element.420, ...), kind=kOutput, calls=%fused_computation.10.clone.1 | convolution fusion | flops 274202624 | bytes 6701056 | tf_op jit(solution)/shard_map/while/body/eval_jaxpr/hgqk,khd->hgqd/dot_general | solution.py:62
  95.1 1.9 %collective-permute-start = (bf16[2,512,128]{2,1,0:T(8,128)(2,1)S(1)}, bf16[2,512,128]{2,1,0:T(8,128)(2,1)S(1)}, u32[]{:S(2)}, u32[]{:S(2)}) collective-permute-start(bf16[2,512,128]{2,1,0:T(8,128)(2,1)S(1)} %get-tuple-element.433), channel_id=1, source_target_pairs={{0,8},{8,16},{16,24},{24,32},{32,40},{40,48},{48,56},{56,64},{64,7... | collective-permute-start | bytes 786440 | tf_op jit(solution)/shard_map/while/body/eval_jaxpr/ppermute | solution.py:21
  97.4 9.2 %collective-permute-done = bf16[2,512,128]{2,1,0:T(8,128)(2,1)S(1)} collective-permute-done((bf16[2,512,128]{2,1,0:T(8,128)(2,1)S(1)}, bf16[2,512,128]{2,1,0:T(8,128)(2,1)S(1)}, u32[]{:S(2)}, u32[]{:S(2)}) %collective-permute-start) | collective-permute-done | bytes 262176 | tf_op jit(solution)/shard_map/while/body/eval_jaxpr/ppermute | solution.py:21
  106.6 0.9 fusion.61
  107.5 1.0 fusion.63
  108.6 1.9 %fusion.64 = f32[1,4,512,128]{3,2,1,0:T(8,128)S(1)} fusion(f32[512,512,4]{1,0,2:T(8,128)S(1)} %get-tuple-element.419, f32[4,512]{1,0:T(4,128)S(1)} %bitcast.138, pred[512,512]{0,1:T(8,128)(4,1)S(1)} %and_and_fusion.3, f32[1,4,512,128]{3,2,1,0:T(8,128)S(1)} %get-tuple-element.436, f32[4,512]{1,0:T(4,128)S(1)} %get-tuple-element.420, ...), kind=kOutput, calls=%fused_computation.10.clone.1 | convolution fusion | flops 274202624 | bytes 6701056 | tf_op jit(solution)/shard_map/while/body/eval_jaxpr/hgqk,khd->hgqd/dot_general | solution.py:62
  110.6 1.9 %collective-permute-start = (bf16[2,512,128]{2,1,0:T(8,128)(2,1)S(1)}, bf16[2,512,128]{2,1,0:T(8,128)(2,1)S(1)}, u32[]{:S(2)}, u32[]{:S(2)}) collective-permute-start(bf16[2,512,128]{2,1,0:T(8,128)(2,1)S(1)} %get-tuple-element.433), channel_id=1, source_target_pairs={{0,8},{8,16},{16,24},{24,32},{32,40},{40,48},{48,56},{56,64},{64,7... | collective-permute-start | bytes 786440 | tf_op jit(solution)/shard_map/while/body/eval_jaxpr/ppermute | solution.py:21
  113.0 9.2 %collective-permute-done = bf16[2,512,128]{2,1,0:T(8,128)(2,1)S(1)} collective-permute-done((bf16[2,512,128]{2,1,0:T(8,128)(2,1)S(1)}, bf16[2,512,128]{2,1,0:T(8,128)(2,1)S(1)}, u32[]{:S(2)}, u32[]{:S(2)}) %collective-permute-start) | collective-permute-done | bytes 262176 | tf_op jit(solution)/shard_map/while/body/eval_jaxpr/ppermute | solution.py:21
  122.2 0.9 fusion.61
  123.1 1.0 fusion.63
  124.2 1.9 %fusion.64 = f32[1,4,512,128]{3,2,1,0:T(8,128)S(1)} fusion(f32[512,512,4]{1,0,2:T(8,128)S(1)} %get-tuple-element.419, f32[4,512]{1,0:T(4,128)S(1)} %bitcast.138, pred[512,512]{0,1:T(8,128)(4,1)S(1)} %and_and_fusion.3, f32[1,4,512,128]{3,2,1,0:T(8,128)S(1)} %get-tuple-element.436, f32[4,512]{1,0:T(4,128)S(1)} %get-tuple-element.420, ...), kind=kOutput, calls=%fused_computation.10.clone.1 | convolution fusion | flops 274202624 | bytes 6701056 | tf_op jit(solution)/shard_map/while/body/eval_jaxpr/hgqk,khd->hgqd/dot_general | solution.py:62
  126.1 1.9 %collective-permute-start = (bf16[2,512,128]{2,1,0:T(8,128)(2,1)S(1)}, bf16[2,512,128]{2,1,0:T(8,128)(2,1)S(1)}, u32[]{:S(2)}, u32[]{:S(2)}) collective-permute-start(bf16[2,512,128]{2,1,0:T(8,128)(2,1)S(1)} %get-tuple-element.433), channel_id=1, source_target_pairs={{0,8},{8,16},{16,24},{24,32},{32,40},{40,48},{48,56},{56,64},{64,7... | collective-permute-start | bytes 786440 | tf_op jit(solution)/shard_map/while/body/eval_jaxpr/ppermute | solution.py:21
  128.5 9.2 %collective-permute-done = bf16[2,512,128]{2,1,0:T(8,128)(2,1)S(1)} collective-permute-done((bf16[2,512,128]{2,1,0:T(8,128)(2,1)S(1)}, bf16[2,512,128]{2,1,0:T(8,128)(2,1)S(1)}, u32[]{:S(2)}, u32[]{:S(2)}) %collective-permute-start) | collective-permute-done | bytes 262176 | tf_op jit(solution)/shard_map/while/body/eval_jaxpr/ppermute | solution.py:21
  137.7 0.9 fusion.61
  138.6 1.0 fusion.63
  139.7 1.9 %fusion.64 = f32[1,4,512,128]{3,2,1,0:T(8,128)S(1)} fusion(f32[512,512,4]{1,0,2:T(8,128)S(1)} %get-tuple-element.419, f32[4,512]{1,0:T(4,128)S(1)} %bitcast.138, pred[512,512]{0,1:T(8,128)(4,1)S(1)} %and_and_fusion.3, f32[1,4,512,128]{3,2,1,0:T(8,128)S(1)} %get-tuple-element.436, f32[4,512]{1,0:T(4,128)S(1)} %get-tuple-element.420, ...), kind=kOutput, calls=%fused_computation.10.clone.1 | convolution fusion | flops 274202624 | bytes 6701056 | tf_op jit(solution)/shard_map/while/body/eval_jaxpr/hgqk,khd->hgqd/dot_general | solution.py:62
  142.6 14.5 %all_to_all.16 = bf16[8,64,512]{2,1,0:T(8,128)(2,1)S(1)} all-to-all(bf16[8,64,512]{2,1,0:T(8,128)(2,1)S(1)} %convert_element_type.41), channel_id=1, replica_groups=mesh['seq'=64,'head'=8] {'head'}, dimensions={0} | all-to-all | bytes 1048576 | tf_op jit(solution)/shard_map/all_to_all | solution.py:94
  157.1 0.8 copy.35
  (91 shorter events, 6.4 us)
Async XLA Ops:
  2.6 4.2 %copy-start.2 = (bf16[512,128]{1,0:T(8,128)(2,1)S(1)}, bf16[512,128]{1,0:T(8,128)(2,1)}, u32[]{:S(2)}) copy-start(bf16[512,128]{1,0:T(8,128)(2,1)} %param.8) | copy-start | bytes 393220
  4.6 1.9 %copy-start = (f32[512,512,4]{1,0,2:T(8,128)}, f32[512,512,4]{1,0,2:T(8,128)S(1)}, u32[]{:S(2)}) copy-start(f32[512,512,4]{1,0,2:T(8,128)S(1)} %get-tuple-element.351) | copy-start | bytes 12582916
  6.9 3.7 %copy-start.1 = (bf16[512,128]{1,0:T(8,128)(2,1)S(1)}, bf16[512,128]{1,0:T(8,128)(2,1)}, u32[]{:S(2)}) copy-start(bf16[512,128]{1,0:T(8,128)(2,1)} %param.7) | copy-start | bytes 393220
  10.6 17.1 %collective-permute-start = (bf16[2,512,128]{2,1,0:T(8,128)(2,1)S(1)}, bf16[2,512,128]{2,1,0:T(8,128)(2,1)S(1)}, u32[]{:S(2)}, u32[]{:S(2)}) collective-permute-start(bf16[2,512,128]{2,1,0:T(8,128)(2,1)S(1)} %get-tuple-element.433), channel_id=1, source_target_pairs={{0,8},{8,16},{16,24},{24,32},{32,40},{40,48},{48,56},{56,64},{64,7... | collective-permute-start | bytes 786440 | tf_op jit(solution)/shard_map/while/body/eval_jaxpr/ppermute | solution.py:21
  31.7 12.7 %collective-permute-start = (bf16[2,512,128]{2,1,0:T(8,128)(2,1)S(1)}, bf16[2,512,128]{2,1,0:T(8,128)(2,1)S(1)}, u32[]{:S(2)}, u32[]{:S(2)}) collective-permute-start(bf16[2,512,128]{2,1,0:T(8,128)(2,1)S(1)} %get-tuple-element.433), channel_id=1, source_target_pairs={{0,8},{8,16},{16,24},{24,32},{32,40},{40,48},{48,56},{56,64},{64,7... | collective-permute-start | bytes 786440 | tf_op jit(solution)/shard_map/while/body/eval_jaxpr/ppermute | solution.py:21
  48.3 11.8 %collective-permute-start = (bf16[2,512,128]{2,1,0:T(8,128)(2,1)S(1)}, bf16[2,512,128]{2,1,0:T(8,128)(2,1)S(1)}, u32[]{:S(2)}, u32[]{:S(2)}) collective-permute-start(bf16[2,512,128]{2,1,0:T(8,128)(2,1)S(1)} %get-tuple-element.433), channel_id=1, source_target_pairs={{0,8},{8,16},{16,24},{24,32},{32,40},{40,48},{48,56},{56,64},{64,7... | collective-permute-start | bytes 786440 | tf_op jit(solution)/shard_map/while/body/eval_jaxpr/ppermute | solution.py:21
  64.0 11.6 %collective-permute-start = (bf16[2,512,128]{2,1,0:T(8,128)(2,1)S(1)}, bf16[2,512,128]{2,1,0:T(8,128)(2,1)S(1)}, u32[]{:S(2)}, u32[]{:S(2)}) collective-permute-start(bf16[2,512,128]{2,1,0:T(8,128)(2,1)S(1)} %get-tuple-element.433), channel_id=1, source_target_pairs={{0,8},{8,16},{16,24},{24,32},{32,40},{40,48},{48,56},{56,64},{64,7... | collective-permute-start | bytes 786440 | tf_op jit(solution)/shard_map/while/body/eval_jaxpr/ppermute | solution.py:21
  79.5 11.6 %collective-permute-start = (bf16[2,512,128]{2,1,0:T(8,128)(2,1)S(1)}, bf16[2,512,128]{2,1,0:T(8,128)(2,1)S(1)}, u32[]{:S(2)}, u32[]{:S(2)}) collective-permute-start(bf16[2,512,128]{2,1,0:T(8,128)(2,1)S(1)} %get-tuple-element.433), channel_id=1, source_target_pairs={{0,8},{8,16},{16,24},{24,32},{32,40},{40,48},{48,56},{56,64},{64,7... | collective-permute-start | bytes 786440 | tf_op jit(solution)/shard_map/while/body/eval_jaxpr/ppermute | solution.py:21
  95.1 11.6 %collective-permute-start = (bf16[2,512,128]{2,1,0:T(8,128)(2,1)S(1)}, bf16[2,512,128]{2,1,0:T(8,128)(2,1)S(1)}, u32[]{:S(2)}, u32[]{:S(2)}) collective-permute-start(bf16[2,512,128]{2,1,0:T(8,128)(2,1)S(1)} %get-tuple-element.433), channel_id=1, source_target_pairs={{0,8},{8,16},{16,24},{24,32},{32,40},{40,48},{48,56},{56,64},{64,7... | collective-permute-start | bytes 786440 | tf_op jit(solution)/shard_map/while/body/eval_jaxpr/ppermute | solution.py:21
  110.6 11.6 %collective-permute-start = (bf16[2,512,128]{2,1,0:T(8,128)(2,1)S(1)}, bf16[2,512,128]{2,1,0:T(8,128)(2,1)S(1)}, u32[]{:S(2)}, u32[]{:S(2)}) collective-permute-start(bf16[2,512,128]{2,1,0:T(8,128)(2,1)S(1)} %get-tuple-element.433), channel_id=1, source_target_pairs={{0,8},{8,16},{16,24},{24,32},{32,40},{40,48},{48,56},{56,64},{64,7... | collective-permute-start | bytes 786440 | tf_op jit(solution)/shard_map/while/body/eval_jaxpr/ppermute | solution.py:21
  126.1 11.6 %collective-permute-start = (bf16[2,512,128]{2,1,0:T(8,128)(2,1)S(1)}, bf16[2,512,128]{2,1,0:T(8,128)(2,1)S(1)}, u32[]{:S(2)}, u32[]{:S(2)}) collective-permute-start(bf16[2,512,128]{2,1,0:T(8,128)(2,1)S(1)} %get-tuple-element.433), channel_id=1, source_target_pairs={{0,8},{8,16},{16,24},{24,32},{32,40},{40,48},{48,56},{56,64},{64,7... | collective-permute-start | bytes 786440 | tf_op jit(solution)/shard_map/while/body/eval_jaxpr/ppermute | solution.py:21
where the time goes:
time: 158 us
  waiting for transfers between devices  78.1 us (49%)
  matrix products  27.9 us (18%)
  starting transfers between devices  17.7 us (11%)
  blocking collectives  14.5 us (9%)
  other arithmetic  14 us (9%)
  local copies, waits for them, and re-layouts  4.72 us (3%)
    ppermute x8, waiting for transfers between devices, shifted(): return lax.ppermute(block, axis, route)  78.1 us
    dot_general x9, matrix products, attend(): jnp.einsum('hgqk,khd->hgqd', weights.astype(jnp.bfloat16), value_mat, pre...  19 us
    ppermute x8, starting transfers between devices, shifted(): return lax.ppermute(block, axis, route)  17.7 us
    all_to_all x1, blocking collectives, body(): lax.all_to_all(outputs, 'head', split_axis=0, concat_axis=1, tiled=True)  14.5 us
    reduce_sum x9, other arithmetic, attend(): row_total = row_total * shrink + jnp.sum(weights, axis=-1)  9.37 us
    dot_general x9, matrix products, attend(): jnp.einsum('qhgd,khd->hgqk', query_mat, key_mat, preferred_element_type=j...  8.98 us
  transfers between devices with their start and end apart: 8, of which 8 were waited for; matrix products, arithmetic and copies ran while one was open for 2% of the time, Pallas kernels for 0%

commit v1 on v0

v1 whole, which is shorter than its diff:
```python
import functools
import math

import jax
import jax.numpy as jnp
from jax import lax
from jax.experimental import pallas as pl
from jax.experimental.pallas import tpu as pltpu
from jax.sharding import PartitionSpec as P

HD = 128
B = 128
GROUP = 4
ROWS = 8
PIECES = 4
FAR = 8
CORES = 2
COLS = GROUP * B
EXTRA = 16
LAG = 2

NEG = -1e30
SCALE = math.log2(math.e) / math.sqrt(HD)
MESH = pl.DeviceIdType.MESH


def kernel(
    n_seq,
    n_head,
    q_hbm,
    k_hbm,
    v_hbm,
    doc_hbm,
    out_ref,
    q_in,
    v_in,
    doc_in,
    q_t,
    kv,
    top,
    acc,
    reach,
    out_buf,
    load_sem,
    send_sem,
    recv_sem,
    out_send,
    out_recv,
):
    s = lax.axis_index("seq")
    h = lax.axis_index("head")
    z = lax.rem(s, ROWS)
    chips = n_head // CORES
    x = h // CORES

    def ring(distance):
        return lax.rem(s + distance + n_seq, n_seq)

    after, before = ring(1), ring(-1)
    up, down = ring(ROWS), ring(-ROWS)
    first_col = ring(-(ROWS - 1))
    last_col = ring(ROWS - 1)

    loads = [
        pltpu.make_async_copy(
            k_hbm.at[pl.ds(j * B, B), :], kv.at[0, j, 0], load_sem.at[j]
        )
        for j in range(PIECES)
    ]
    loads.append(pltpu.make_async_copy(v_hbm, v_in, load_sem.at[PIECES]))
    loads.append(pltpu.make_async_copy(doc_hbm, doc_in, load_sem.at[PIECES + 1]))
    loads.append(pltpu.make_async_copy(q_hbm, q_in, load_sem.at[PIECES + 2]))
    for copy in loads:
        copy.start()

    barrier = pltpu.get_barrier_semaphore()

    def greet(to_seq, to_head):
        pl.semaphore_signal(barrier, inc=1, device_id=(to_seq, to_head), device_id_type=MESH)

    for to in (after, before, up, down):
        greet(to, h)
    for step in range(1, n_head):
        greet(s, lax.rem(h + step, n_head))

    @pl.when(z == ROWS - 1)
    def _():
        greet(first_col, h)

    @pl.when(z == 0)
    def _():
        greet(last_col, h)

    for copy in loads[: PIECES + 1]:
        copy.wait()
    for j in range(PIECES):
        kv[0, j, 1] = v_in[pl.ds(j * B, B), :].T

    edge = jnp.where((z == 0) | (z == ROWS - 1), 1, 0)
    pl.semaphore_wait(barrier, 4 + n_head - 1 + edge)

    def move(src, dst, j, to):
        return pltpu.make_async_remote_copy(
            src_ref=kv.at[src, j],
            dst_ref=kv.at[dst, j],
            send_sem=send_sem.at[dst, j],
            recv_sem=recv_sem.at[dst, j],
            device_id=(to, h),
            device_id_type=MESH,
        )

    def send(src, dst, j, to):
        move(src, dst, j, to).start()

    def arrived(d, j):
        move(d, d, j, after).wait_recv()

    def sent(d, j):
        move(d, d, j, after).wait_send()

    for j in range(PIECES):
        send(0, FAR, j, up)

        send(0, 1, j, after)

        @pl.when(z == 0)
        def _():
            send(0, FAR - 1, j, last_col)

    loads[PIECES + 1].wait()
    lengths = doc_in[...]
    count = lengths.shape[1]
    shape = (count, count)
    upto = lax.broadcasted_iota(jnp.int32, shape, 1) <= lax.broadcasted_iota(jnp.int32, shape, 0)
    ends = jnp.sum(
        jnp.where(upto, jnp.broadcast_to(lengths, shape), 0).astype(jnp.float32),
        axis=1,
        keepdims=True,
    ).astype(jnp.int32)
    for i in range(PIECES):
        block = s * PIECES + i
        start = jnp.max(
            jnp.where(ends <= block, ends, 0).astype(jnp.float32), axis=0, keepdims=True
        ).astype(jnp.int32)
        reach[i] = jnp.broadcast_to(block - start, (1, COLS))

    loads[PIECES + 2].wait()
    for i in range(PIECES):
        for g in range(GROUP):
            rows = q_in[i * B : (i + 1) * B, g * HD : (g + 1) * HD]
            scaled = rows.astype(jnp.float32).T * SCALE
            high = scaled.astype(jnp.bfloat16)
            q_t[i, :HD, g * B : (g + 1) * B] = high
            q_t[i, HD:, g * B : (g + 1) * B] = (scaled - high.astype(jnp.float32)).astype(jnp.bfloat16)

    def update(i, chunks, first=False):
        queries = q_t[i]
        far = reach[i]
        scores, shown = [], []
        for d, blocks in chunks:
            n = len(blocks)
            keys = kv[d, blocks[0] : blocks[0] + n, 0].reshape(n * B, HD)
            pair = jnp.dot(
                jnp.concatenate([keys, keys], axis=1), queries, preferred_element_type=jnp.float32
            )
            for b, j in enumerate(blocks):
                block = pair[b * B : (b + 1) * B]
                delta = PIECES * d + i - j
                if first:
                    key = lax.broadcasted_iota(jnp.int32, (B, COLS), 0) + j * B
                    query = lax.rem(lax.broadcasted_iota(jnp.int32, (B, COLS), 1), B) + i * B
                    block = jnp.where(key <= query, block, NEG)
                    shown.append((delta <= far) & (delta >= 0))
                else:
                    shown.append(delta <= far)
                scores.append(block)
        peak = None
        for block, show in zip(scores, shown):
            here = jnp.where(show, jnp.max(block, axis=0, keepdims=True), NEG)
            peak = here if peak is None else jnp.maximum(peak, here)
        if not first:
            old = top[i]
            peak = jnp.maximum(old, peak)
            shrink = jnp.exp2(old - peak)
        top[i] = peak
        added = None
        at = 0
        ones = jnp.ones((EXTRA, B), jnp.bfloat16)
        for d, blocks in chunks:
            n = len(blocks)
            weights = [
                jnp.exp2(block - jnp.where(show, peak, -NEG)).astype(jnp.bfloat16)
                for block, show in zip(scores[at : at + n], shown[at : at + n])
            ]
            at += n
            values = jnp.concatenate(
                [jnp.concatenate([kv[d, j, 1], ones], axis=0) for j in blocks], axis=1
            )
            part = jnp.dot(
                values, jnp.concatenate(weights, axis=0), preferred_element_type=jnp.float32
            )
            added = part if added is None else added + part
        acc[i] = added if first else acc[i] * shrink + added

    every = tuple(range(PIECES))
    half = PIECES // 2

    @pl.loop(0, PIECES)
    def _(j):
        update(j, [(0, every)], first=True)

    far_steps = 4 * PIECES
    work_from = PIECES - 1 + LAG

    @pl.loop(0, 3 * PIECES + work_from)
    def _(t):
        j = lax.rem(t, PIECES)
        d = FAR - t // PIECES

        @pl.when(t < far_steps)
        def _():
            arrived(d, j)

            @pl.when((d > 5) & ((d < FAR) | (z != 0)))
            def _():
                send(d, d - 1, j, before)

        u = t - LAG
        near = u // PIECES + 1
        k = lax.rem(u + PIECES, PIECES)

        @pl.when(u >= 0)
        def _():
            arrived(near, k)

            @pl.when(near < 4)
            def _():
                send(near, near + 1, k, after)

        w = t - work_from

        @pl.when(w >= 0)
        def _():
            p = w // PIECES + 1
            update(lax.rem(w, PIECES), [(p, every), (FAR + 1 - p, every)])

    @pl.loop(0, PIECES)
    def _(j):
        update(j, [(5, every[:half]), (4, every[:half])])

    for u in range(3 * PIECES + work_from - LAG, 4 * PIECES):
        arrived(u // PIECES + 1, u % PIECES)

    own = pltpu.make_async_copy(
        out_buf.at[h],
        out_ref.at[:, pl.ds(pl.multiple_of(h * COLS, COLS), COLS)],
        load_sem.at[0],
    )
    for hop in (2, 1, 3, 0):
        to_x = lax.rem(x + hop, chips)
        i = to_x
        update(i, [(5, every[half:]), (4, every[half:])])
        final = acc[i, :HD] * (1.0 / acc[i, HD : HD + 1])
        for g in range(GROUP):
            rows = final[:, g * B : (g + 1) * B].T.astype(jnp.bfloat16)
            for core in range(CORES):
                part = B // CORES
                out_buf[to_x * CORES + core, :, g * HD : (g + 1) * HD] = rows[
                    core * part : (core + 1) * part
                ]
        for core in range(CORES):
            target = to_x * CORES + core
            step = lax.rem(target - h + n_head, n_head)
            there = pltpu.make_async_remote_copy(
                src_ref=out_buf.at[target],
                dst_ref=out_ref.at[:, pl.ds(pl.multiple_of(h * COLS, COLS), COLS)],
                send_sem=out_send.at[target],
                recv_sem=out_recv.at[h],
                device_id=(s, target),
                device_id_type=MESH,
            )
            if hop == 0:

                @pl.when(step != 0)
                def _():
                    there.start()

                @pl.when(step == 0)
                def _():
                    own.start()

            else:
                there.start()

    @pl.loop(1, FAR + 1)
    def _(d):
        @pl.loop(0, PIECES)
        def _(j):
            sent(d, j)

    for step in range(1, n_head):
        peer = lax.rem(h + step, n_head)
        other = pltpu.make_async_remote_copy(
            src_ref=out_buf.at[peer],
            dst_ref=out_ref.at[:, pl.ds(pl.multiple_of(peer * COLS, COLS), COLS)],
            send_sem=out_send.at[peer],
            recv_sem=out_recv.at[peer],
            device_id=(s, peer),
            device_id_type=MESH,
        )
        other.wait_send()
        other.wait_recv()
    own.wait()


def body(n_seq, n_head, queries, key_rows, value_rows, doc_blocks):
    tokens = queries.shape[0]
    part = tokens // n_head
    any_space = pl.BlockSpec(memory_space=pl.ANY)
    bf16, f32 = jnp.bfloat16, jnp.float32
    pairs = tokens * PIECES * FAR * B * GROUP
    return pl.pallas_call(
        functools.partial(kernel, n_seq, n_head),
        out_shape=jax.ShapeDtypeStruct((part, n_head * COLS), bf16),
        in_specs=[any_space] * 4,
        out_specs=any_space,
        scratch_shapes=[
            pltpu.VMEM((tokens, COLS), bf16),
            pltpu.VMEM((tokens, HD), bf16),
            pltpu.VMEM((1, doc_blocks.shape[0]), jnp.int32),
            pltpu.VMEM((PIECES, 2 * HD, COLS), bf16),
            pltpu.VMEM((FAR + 1, PIECES, 2, B, HD), bf16),
            pltpu.VMEM((PIECES, 1, COLS), f32),
            pltpu.VMEM((PIECES, HD + EXTRA, COLS), f32),
            pltpu.VMEM((PIECES, 1, COLS), jnp.int32),
            pltpu.VMEM((n_head, part, COLS), bf16),
            pltpu.SemaphoreType.DMA((PIECES + 3,)),
            pltpu.SemaphoreType.DMA((FAR + 1, PIECES)),
            pltpu.SemaphoreType.DMA((FAR + 1, PIECES)),
            pltpu.SemaphoreType.DMA((n_head,)),
            pltpu.SemaphoreType.DMA((n_head,)),
        ],
        compiler_params=pltpu.CompilerParams(
            collective_id=0, has_side_effects=True, vmem_limit_bytes=62 << 20
        ),
        cost_estimate=pl.CostEstimate(
            flops=4 * pairs * HD, bytes_accessed=2 << 20, transcendentals=pairs
        ),
        name="attend",
    )(queries, key_rows, value_rows, doc_blocks.reshape(1, -1))


def solution(mesh):
    in_specs = (P("seq", "head"), P("seq", "head"), P("seq", "head"), P())
    out_specs = P(("seq", "head"), None)
    return jax.shard_map(
        functools.partial(body, mesh.shape["seq"], mesh.shape["head"]),
        mesh=mesh,
        in_specs=in_specs,
        out_specs=out_specs,
        check_vma=False,
    )
```

time: 158 us -> 58.7 us (0.37)
  the two profiles are of different devices: /device:TPU:32 before, /device:TPU:1 now
where the time goes in v1:
time: 58.7 us; the launch traced here: 58.5 us
  Pallas kernels  56.6 us (96%)
  local copies, waits for them, and re-layouts  1.87 us (3%)
    pallas_call x1, Pallas kernels, body(): pl.pallas_call(functools.partial(kernel, n_seq, n_head), out_shape=jax.Sh...  56.6 us
    unnamed x1, local copies, waits for them, and re-layouts  1.87 us

profile of v1, /device:TPU:1, one launch (start us, length us, event | category | flops | bytes accessed | tf_op | source)
XLA Modules:
  0.0 58.5 jit_solution(16837525060121311123)
XLA Ops:
  0.0 56.6 %attend.1 = bf16[64,4096]{1,0:T(8,128)(2,1)} custom-call(bf16[512,512]{1,0:T(8,128)(2,1)} %q_hbm.1, bf16[512,128]{1,0:T(8,128)(2,1)} %k_hbm.1, bf16[512,128]{1,0:T(8,128)(2,1)} %v_hbm.1, s32[1,32]{1,0:T(1,128)} %bitcast.1), custom_call_target="tpu_custom_call" | custom-call | flops 4294967296 | bytes 2097152 | tf_op jit(solution)/shard_map/attend/pallas_call | solution.py:322
  56.7 1.9 %copy.6 = bf16[64,4096]{1,0:T(8,128)(2,1)} copy(bf16[64,4096]{1,0:T(8,128)(2,1)} %attend.1) | data formatting | bytes 1048576

commit v2 on v1

--- a/solution.py
+++ b/solution.py
@@ -17,7 +17,8 @@
 CORES = 2
 COLS = GROUP * B
 EXTRA = 16
-LAG = 2
+WINDOW = 2
+SHARE = 1
 
 NEG = -1e30
 SCALE = math.log2(math.e) / math.sqrt(HD)
@@ -41,11 +42,13 @@
     acc,
     reach,
     out_buf,
+    relay_buf,
     load_sem,
     send_sem,
     recv_sem,
     out_send,
     out_recv,
+    relay_sem,
 ):
     s = lax.axis_index("seq")
     h = lax.axis_index("head")
@@ -58,8 +61,7 @@
 
     after, before = ring(1), ring(-1)
     up, down = ring(ROWS), ring(-ROWS)
-    first_col = ring(-(ROWS - 1))
-    last_col = ring(ROWS - 1)
+    ahead, behind = ring(ROWS - 1), ring(1 - ROWS)
 
     loads = [
         pltpu.make_async_copy(
@@ -78,26 +80,17 @@
     def greet(to_seq, to_head):
         pl.semaphore_signal(barrier, inc=1, device_id=(to_seq, to_head), device_id_type=MESH)
 
-    for to in (after, before, up, down):
+    for to in (after, before, up, down, ahead, behind):
         greet(to, h)
     for step in range(1, n_head):
         greet(s, lax.rem(h + step, n_head))
-
-    @pl.when(z == ROWS - 1)
-    def _():
-        greet(first_col, h)
-
-    @pl.when(z == 0)
-    def _():
-        greet(last_col, h)
 
     for copy in loads[: PIECES + 1]:
         copy.wait()
     for j in range(PIECES):
         kv[0, j, 1] = v_in[pl.ds(j * B, B), :].T
 
-    edge = jnp.where((z == 0) | (z == ROWS - 1), 1, 0)
-    pl.semaphore_wait(barrier, 4 + n_head - 1 + edge)
+    pl.semaphore_wait(barrier, 6 + n_head - 1)
 
     def move(src, dst, j, to):
         return pltpu.make_async_remote_copy(
@@ -118,14 +111,19 @@
     def sent(d, j):
         move(d, d, j, after).wait_send()
 
-    for j in range(PIECES):
-        send(0, FAR, j, up)
-
+    whole = 3 * PIECES
+    n_forward = whole + SHARE
+    n_backward = whole + PIECES - SHARE
+
+    def forward(n):
+        return 1 + n // PIECES, lax.rem(n, PIECES)
+
+    def backward(n):
+        return FAR - 1 - n // PIECES, lax.rem(n, PIECES) + jnp.where(n >= whole, SHARE, 0)
+
+    for j in range(WINDOW):
         send(0, 1, j, after)
-
-        @pl.when(z == 0)
-        def _():
-            send(0, FAR - 1, j, last_col)
+        send(0, FAR - 1, j, ahead)
 
     loads[PIECES + 1].wait()
     lengths = doc_in[...]
@@ -203,127 +201,171 @@
         acc[i] = added if first else acc[i] * shrink + added
 
     every = tuple(range(PIECES))
-    half = PIECES // 2
-
-    @pl.loop(0, PIECES)
-    def _(j):
-        update(j, [(0, every)], first=True)
-
-    far_steps = 4 * PIECES
-    work_from = PIECES - 1 + LAG
-
-    @pl.loop(0, 3 * PIECES + work_from)
+
+    late = PIECES - WINDOW
+    turn = whole - WINDOW
+    first_pair = PIECES + late - 1
+    steps = first_pair + whole
+    leaf = first_pair
+    leaf_work = leaf + PIECES + 1
+
+    @pl.loop(0, steps)
     def _(t):
-        j = lax.rem(t, PIECES)
-        d = FAR - t // PIECES
-
-        @pl.when(t < far_steps)
-        def _():
-            arrived(d, j)
-
-            @pl.when((d > 5) & ((d < FAR) | (z != 0)))
+        n = t + WINDOW
+
+        @pl.when(t < n_forward)
+        def _():
+            sent(*forward(t))
+
+        @pl.when((t >= late) & (t - late < n_forward))
+        def _():
+            arrived(*forward(t - late))
+
+        @pl.when(n < PIECES)
+        def _():
+            send(0, 1, n, after)
+
+        @pl.when((n >= PIECES) & (n < n_forward))
+        def _():
+            d, j = forward(n)
+            send(d - 1, d, j, after)
+
+        @pl.when(t < n_backward)
+        def _():
+            sent(*backward(t))
+
+        @pl.when((t >= late) & (t <= turn))
+        def _():
+            arrived(*backward(t - late))
+
+        for k in range(SHARE):
+
+            @pl.when((t == turn) if k + 1 < SHARE else ((t >= turn) & (t < n_backward)))
             def _():
-                send(d, d - 1, j, before)
-
-        u = t - LAG
-        near = u // PIECES + 1
-        k = lax.rem(u + PIECES, PIECES)
-
-        @pl.when(u >= 0)
-        def _():
-            arrived(near, k)
-
-            @pl.when(near < 4)
-            def _():
-                send(near, near + 1, k, after)
-
-        w = t - work_from
-
-        @pl.when(w >= 0)
-        def _():
-            p = w // PIECES + 1
-            update(lax.rem(w, PIECES), [(p, every), (FAR + 1 - p, every)])
-
-    @pl.loop(0, PIECES)
-    def _(j):
-        update(j, [(5, every[:half]), (4, every[:half])])
-
-    for u in range(3 * PIECES + work_from - LAG, 4 * PIECES):
-        arrived(u // PIECES + 1, u % PIECES)
-
-    own = pltpu.make_async_copy(
-        out_buf.at[h],
-        out_ref.at[:, pl.ds(pl.multiple_of(h * COLS, COLS), COLS)],
-        load_sem.at[0],
+                arrived(*backward(t - late + 1 + k))
+
+        @pl.when(n < PIECES)
+        def _():
+            send(0, FAR - 1, n, ahead)
+
+        @pl.when((n >= PIECES) & (n < n_backward))
+        def _():
+            d, j = backward(n)
+            send(d + 1, d, j, before)
+
+        @pl.when((t > leaf) & (t < leaf + PIECES - 1))
+        def _():
+            sent(FAR, t - leaf)
+
+        @pl.when((t >= leaf) & (t < leaf + PIECES - 1))
+        def _():
+            send(0, FAR, t - leaf + 1, up)
+
+        @pl.when(t < PIECES)
+        def _():
+            update(t, [(0, every)], first=True)
+
+        @pl.when(t >= first_pair)
+        def _():
+            m = 1 + (t - first_pair) // PIECES
+            update(lax.rem(t - first_pair, PIECES), [(FAR - m, every), (m, every)])
+
+        @pl.when(t == leaf_work)
+        def _():
+            for j in range(1, PIECES):
+                arrived(FAR, j)
+
+        @pl.when((t >= leaf_work) & (t < leaf_work + PIECES))
+        def _():
+            update(t - leaf_work, [(FAR, every[1:])])
+
+    sent(FAR, PIECES - 1)
+
+    for n in range(n_backward - late + SHARE, n_backward):
+        arrived(*backward(n))
+
+    def columns(who):
+        return pl.ds(pl.multiple_of(who * COLS, COLS), COLS)
+
+    own = pltpu.make_async_copy(out_buf.at[h], out_ref.at[:, columns(h)], load_sem.at[0])
+    core_here = lax.rem(h, CORES)
+
+    def chip(hop):
+        return lax.rem(x + hop, chips)
+
+    def deliver(src, whose, target, send_at):
+        return pltpu.make_async_remote_copy(
+            src_ref=src,
+            dst_ref=out_ref.at[:, columns(whose)],
+            send_sem=send_at,
+            recv_sem=out_recv.at[whose],
+            device_id=(s, target),
+            device_id_type=MESH,
+        )
+
+    relay_in = pltpu.make_async_remote_copy(
+        src_ref=out_buf.at[chip(2) * CORES + 1],
+        dst_ref=relay_buf,
+        send_sem=out_send.at[chip(2) * CORES + 1],
+        recv_sem=relay_sem.at[0],
+        device_id=(s, chip(chips - 1) * CORES + core_here),
+        device_id_type=MESH,
     )
-    for hop in (2, 1, 3, 0):
-        to_x = lax.rem(x + hop, chips)
-        i = to_x
-        update(i, [(5, every[half:]), (4, every[half:])])
+    relay_out = deliver(
+        relay_buf, chip(1) * CORES + core_here, chip(chips - 1) * CORES + 1, relay_sem.at[1]
+    )
+
+    for hop in (2, 3, 1, 0):
+        i = chip(hop)
+        update(i, [(4, every)])
         final = acc[i, :HD] * (1.0 / acc[i, HD : HD + 1])
         for g in range(GROUP):
             rows = final[:, g * B : (g + 1) * B].T.astype(jnp.bfloat16)
             for core in range(CORES):
                 part = B // CORES
-                out_buf[to_x * CORES + core, :, g * HD : (g + 1) * HD] = rows[
+                out_buf[i * CORES + core, :, g * HD : (g + 1) * HD] = rows[
                     core * part : (core + 1) * part
                 ]
         for core in range(CORES):
-            target = to_x * CORES + core
-            step = lax.rem(target - h + n_head, n_head)
-            there = pltpu.make_async_remote_copy(
-                src_ref=out_buf.at[target],
-                dst_ref=out_ref.at[:, pl.ds(pl.multiple_of(h * COLS, COLS), COLS)],
-                send_sem=out_send.at[target],
-                recv_sem=out_recv.at[h],
-                device_id=(s, target),
-                device_id_type=MESH,
-            )
-            if hop == 0:
-
-                @pl.when(step != 0)
+            target = i * CORES + core
+            there = deliver(out_buf.at[target], h, target, out_send.at[target])
+            if hop == 2 and core == 1:
+                relay_in.start()
+            elif hop:
+                there.start()
+            else:
+
+                @pl.when(core_here != core)
                 def _():
                     there.start()
 
-                @pl.when(step == 0)
+                @pl.when(core_here == core)
                 def _():
                     own.start()
 
-            else:
-                there.start()
-
-    @pl.loop(1, FAR + 1)
-    def _(d):
-        @pl.loop(0, PIECES)
-        def _(j):
-            sent(d, j)
+    relay_in.wait_recv()
+    relay_out.start()
 
     for step in range(1, n_head):
         peer = lax.rem(h + step, n_head)
-        other = pltpu.make_async_remote_copy(
-            src_ref=out_buf.at[peer],
-            dst_ref=out_ref.at[:, pl.ds(pl.multiple_of(peer * COLS, COLS), COLS)],
-            send_sem=out_send.at[peer],
-            recv_sem=out_recv.at[peer],
-            device_id=(s, peer),
-            device_id_type=MESH,
-        )
+        other = deliver(out_buf.at[peer], peer, peer, out_send.at[peer])
         other.wait_send()
         other.wait_recv()
+    relay_out.wait_send()
     own.wait()
 
 
 def body(n_seq, n_head, queries, key_rows, value_rows, doc_blocks):
     tokens = queries.shape[0]
     part = tokens // n_head
-    any_space = pl.BlockSpec(memory_space=pl.ANY)
+    in_hbm = pl.BlockSpec(memory_space=pltpu.HBM)
     bf16, f32 = jnp.bfloat16, jnp.float32
     pairs = tokens * PIECES * FAR * B * GROUP
     return pl.pallas_call(
         functools.partial(kernel, n_seq, n_head),
         out_shape=jax.ShapeDtypeStruct((part, n_head * COLS), bf16),
-        in_specs=[any_space] * 4,
-        out_specs=any_space,
+        in_specs=[in_hbm] * 4,
+        out_specs=pl.BlockSpec(memory_space=pl.ANY),
         scratch_shapes=[
             pltpu.VMEM((tokens, COLS), bf16),
             pltpu.VMEM((tokens, HD), bf16),
@@ -334,11 +376,13 @@
             pltpu.VMEM((PIECES, HD + EXTRA, COLS), f32),
             pltpu.VMEM((PIECES, 1, COLS), jnp.int32),
             pltpu.VMEM((n_head, part, COLS), bf16),
+            pltpu.VMEM((part, COLS), bf16),
             pltpu.SemaphoreType.DMA((PIECES + 3,)),
             pltpu.SemaphoreType.DMA((FAR + 1, PIECES)),
             pltpu.SemaphoreType.DMA((FAR + 1, PIECES)),
             pltpu.SemaphoreType.DMA((n_head,)),
             pltpu.SemaphoreType.DMA((n_head,)),
+            pltpu.SemaphoreType.DMA((2,)),
         ],
         compiler_params=pltpu.CompilerParams(
             collective_id=0, has_side_effects=True, vmem_limit_bytes=62 << 20

time: 58.7 us -> 61.1 us (1.041)
  Pallas kernels: 56.6 us -> 59.1 us
    pallas_call x1, Pallas kernels: 56.6 us -> 59.1 us  [body(): pl.pallas_call(functools.partial(kernel, n_seq, n_head), out_shape=jax.Sh...]
where the time goes in v2:
time: 61.1 us; the launch traced here: 61 us
  Pallas kernels  59.1 us (97%)
  local copies, waits for them, and re-layouts  1.87 us (3%)
    pallas_call x1, Pallas kernels, body(): pl.pallas_call(functools.partial(kernel, n_seq, n_head), out_shape=jax.Sh...  59.1 us
    unnamed x1, local copies, waits for them, and re-layouts  1.87 us

profile of v2, /device:TPU:1, one launch (start us, length us, event | category | flops | bytes accessed | tf_op | source)
XLA Modules:
  0.0 61.0 jit_solution(4903980865399250246)
XLA Ops:
  0.0 59.1 %attend.1 = bf16[64,4096]{1,0:T(8,128)(2,1)} custom-call(bf16[512,512]{1,0:T(8,128)(2,1)} %q_hbm.1, bf16[512,128]{1,0:T(8,128)(2,1)} %k_hbm.1, bf16[512,128]{1,0:T(8,128)(2,1)} %v_hbm.1, s32[1,32]{1,0:T(1,128)} %bitcast.1), custom_call_target="tpu_custom_call" | custom-call | flops 4294967296 | bytes 2097152 | tf_op jit(solution)/shard_map/attend/pallas_call | solution.py:364
  59.1 1.9 %copy.6 = bf16[64,4096]{1,0:T(8,128)(2,1)} copy(bf16[64,4096]{1,0:T(8,128)(2,1)} %attend.1) | data formatting | bytes 1048576

commit v3 on v2

--- a/solution.py
+++ b/solution.py
@@ -18,7 +18,6 @@
 COLS = GROUP * B
 EXTRA = 16
 WINDOW = 2
-SHARE = 1
 
 NEG = -1e30
 SCALE = math.log2(math.e) / math.sqrt(HD)
@@ -112,14 +111,15 @@
         move(d, d, j, after).wait_send()
 
     whole = 3 * PIECES
-    n_forward = whole + SHARE
-    n_backward = whole + PIECES - SHARE
+    longest = 4 * PIECES
+    forward_end = jnp.where(z == ROWS - 2, longest, whole)
+    backward_end = jnp.where(z == 0, whole, longest)
 
     def forward(n):
         return 1 + n // PIECES, lax.rem(n, PIECES)
 
     def backward(n):
-        return FAR - 1 - n // PIECES, lax.rem(n, PIECES) + jnp.where(n >= whole, SHARE, 0)
+        return FAR - 1 - n // PIECES, lax.rem(n, PIECES)
 
     for j in range(WINDOW):
         send(0, 1, j, after)
@@ -203,52 +203,46 @@
     every = tuple(range(PIECES))
 
     late = PIECES - WINDOW
-    turn = whole - WINDOW
     first_pair = PIECES + late - 1
     steps = first_pair + whole
-    leaf = first_pair
-    leaf_work = leaf + PIECES + 1
+    leaf_work = steps - PIECES
+    leaf = leaf_work - PIECES - 1
 
     @pl.loop(0, steps)
     def _(t):
         n = t + WINDOW
-
-        @pl.when(t < n_forward)
+        here = t - late
+
+        @pl.when(t < forward_end)
         def _():
             sent(*forward(t))
 
-        @pl.when((t >= late) & (t - late < n_forward))
-        def _():
-            arrived(*forward(t - late))
+        @pl.when((here >= 0) & (here < whole))
+        def _():
+            arrived(*forward(here))
 
         @pl.when(n < PIECES)
         def _():
             send(0, 1, n, after)
 
-        @pl.when((n >= PIECES) & (n < n_forward))
+        @pl.when((n >= PIECES) & (n < forward_end))
         def _():
             d, j = forward(n)
             send(d - 1, d, j, after)
 
-        @pl.when(t < n_backward)
+        @pl.when(t < backward_end)
         def _():
             sent(*backward(t))
 
-        @pl.when((t >= late) & (t <= turn))
-        def _():
-            arrived(*backward(t - late))
-
-        for k in range(SHARE):
-
-            @pl.when((t == turn) if k + 1 < SHARE else ((t >= turn) & (t < n_backward)))
-            def _():
-                arrived(*backward(t - late + 1 + k))
+        @pl.when((here >= 0) & (here < whole))
+        def _():
+            arrived(*backward(here))
 
         @pl.when(n < PIECES)
         def _():
             send(0, FAR - 1, n, ahead)
 
-        @pl.when((n >= PIECES) & (n < n_backward))
+        @pl.when((n >= PIECES) & (n < backward_end))
         def _():
             d, j = backward(n)
             send(d + 1, d, j, before)
@@ -275,14 +269,13 @@
             for j in range(1, PIECES):
                 arrived(FAR, j)
 
-        @pl.when((t >= leaf_work) & (t < leaf_work + PIECES))
+        @pl.when(t >= leaf_work)
         def _():
             update(t - leaf_work, [(FAR, every[1:])])
 
     sent(FAR, PIECES - 1)
-
-    for n in range(n_backward - late + SHARE, n_backward):
-        arrived(*backward(n))
+    for j in every:
+        arrived(4, j)
 
     def columns(who):
         return pl.ds(pl.multiple_of(who * COLS, COLS), COLS)
@@ -308,14 +301,14 @@
         dst_ref=relay_buf,
         send_sem=out_send.at[chip(2) * CORES + 1],
         recv_sem=relay_sem.at[0],
-        device_id=(s, chip(chips - 1) * CORES + core_here),
+        device_id=(s, chip(1) * CORES + core_here),
         device_id_type=MESH,
     )
     relay_out = deliver(
-        relay_buf, chip(1) * CORES + core_here, chip(chips - 1) * CORES + 1, relay_sem.at[1]
+        relay_buf, chip(chips - 1) * CORES + core_here, chip(1) * CORES + 1, relay_sem.at[1]
     )
 
-    for hop in (2, 3, 1, 0):
+    for hop in (2, 1, 3, 0):
         i = chip(hop)
         update(i, [(4, every)])
         final = acc[i, :HD] * (1.0 / acc[i, HD : HD + 1])

time: 61.1 us -> 60.7 us (level)
  no operation moved by 1% of the time
where the time goes in v3:
time: 60.7 us; the launch traced here: 60.5 us
  Pallas kernels  58.6 us (97%)
  local copies, waits for them, and re-layouts  1.87 us (3%)
    pallas_call x1, Pallas kernels, body(): pl.pallas_call(functools.partial(kernel, n_seq, n_head), out_shape=jax.Sh...  58.6 us
    unnamed x1, local copies, waits for them, and re-layouts  1.87 us

profile of v3, /device:TPU:1, one launch (start us, length us, event | category | flops | bytes accessed | tf_op | source)
XLA Modules:
  0.0 60.5 jit_solution(6240625475341065797)
XLA Ops:
  0.0 58.6 %attend.1 = bf16[64,4096]{1,0:T(8,128)(2,1)} custom-call(bf16[512,512]{1,0:T(8,128)(2,1)} %q_hbm.1, bf16[512,128]{1,0:T(8,128)(2,1)} %k_hbm.1, bf16[512,128]{1,0:T(8,128)(2,1)} %v_hbm.1, s32[1,32]{1,0:T(1,128)} %bitcast.1), custom_call_target="tpu_custom_call" | custom-call | flops 4294967296 | bytes 2097152 | tf_op jit(solution)/shard_map/attend/pallas_call | solution.py:357
  58.6 1.9 %copy.6 = bf16[64,4096]{1,0:T(8,128)(2,1)} copy(bf16[64,4096]{1,0:T(8,128)(2,1)} %attend.1) | data formatting | bytes 1048576

commit v4 on v1

--- a/solution.py
+++ b/solution.py
@@ -17,6 +17,7 @@
 CORES = 2
 COLS = GROUP * B
 EXTRA = 16
+HALF = COLS // 2
 LAG = 2
 
 NEG = -1e30
@@ -154,53 +155,55 @@
             q_t[i, HD:, g * B : (g + 1) * B] = (scaled - high.astype(jnp.float32)).astype(jnp.bfloat16)
 
     def update(i, chunks, first=False):
-        queries = q_t[i]
-        far = reach[i]
-        scores, shown = [], []
+        far = reach[i][:, :HALF]
+        ones = jnp.ones((EXTRA, B), jnp.bfloat16)
+        keys, values, pairs = [], [], []
         for d, blocks in chunks:
             n = len(blocks)
-            keys = kv[d, blocks[0] : blocks[0] + n, 0].reshape(n * B, HD)
-            pair = jnp.dot(
-                jnp.concatenate([keys, keys], axis=1), queries, preferred_element_type=jnp.float32
+            part = kv[d, blocks[0] : blocks[0] + n, 0].reshape(n * B, HD)
+            keys.append(jnp.concatenate([part, part], axis=1))
+            values.append(
+                jnp.concatenate(
+                    [jnp.concatenate([kv[d, j, 1], ones], axis=0) for j in blocks], axis=1
+                )
             )
-            for b, j in enumerate(blocks):
-                block = pair[b * B : (b + 1) * B]
+            pairs += [(d, j) for j in blocks]
+        keys = jnp.concatenate(keys, axis=0)
+        values = jnp.concatenate(values, axis=1)
+        halves = [slice(c * HALF, (c + 1) * HALF) for c in range(COLS // HALF)]
+        products = [
+            jnp.dot(keys, q_t[i, :, half], preferred_element_type=jnp.float32) for half in halves
+        ]
+        for half, product in zip(halves, products):
+            scores, shown = [], []
+            for b, (d, j) in enumerate(pairs):
+                block = product[b * B : (b + 1) * B]
                 delta = PIECES * d + i - j
+                show = delta <= far
                 if first:
-                    key = lax.broadcasted_iota(jnp.int32, (B, COLS), 0) + j * B
-                    query = lax.rem(lax.broadcasted_iota(jnp.int32, (B, COLS), 1), B) + i * B
+                    key = lax.broadcasted_iota(jnp.int32, (B, HALF), 0) + j * B
+                    query = lax.rem(lax.broadcasted_iota(jnp.int32, (B, HALF), 1), B) + i * B
                     block = jnp.where(key <= query, block, NEG)
-                    shown.append((delta <= far) & (delta >= 0))
-                else:
-                    shown.append(delta <= far)
+                    show = show & (delta >= 0)
+                shown.append(show)
                 scores.append(block)
-        peak = None
-        for block, show in zip(scores, shown):
-            here = jnp.where(show, jnp.max(block, axis=0, keepdims=True), NEG)
-            peak = here if peak is None else jnp.maximum(peak, here)
-        if not first:
-            old = top[i]
-            peak = jnp.maximum(old, peak)
-            shrink = jnp.exp2(old - peak)
-        top[i] = peak
-        added = None
-        at = 0
-        ones = jnp.ones((EXTRA, B), jnp.bfloat16)
-        for d, blocks in chunks:
-            n = len(blocks)
+            peak = None
+            for block, show in zip(scores, shown):
+                here = jnp.where(show, jnp.max(block, axis=0, keepdims=True), NEG)
+                peak = here if peak is None else jnp.maximum(peak, here)
+            if not first:
+                old = top[i, :, half]
+                peak = jnp.maximum(old, peak)
+                shrink = jnp.exp2(old - peak)
+            top[i, :, half] = peak
             weights = [
                 jnp.exp2(block - jnp.where(show, peak, -NEG)).astype(jnp.bfloat16)
-                for block, show in zip(scores[at : at + n], shown[at : at + n])
+                for block, show in zip(scores, shown)
             ]
-            at += n
-            values = jnp.concatenate(
-                [jnp.concatenate([kv[d, j, 1], ones], axis=0) for j in blocks], axis=1
-            )
-            part = jnp.dot(
+            added = jnp.dot(
                 values, jnp.concatenate(weights, axis=0), preferred_element_type=jnp.float32
             )
-            added = part if added is None else added + part
-        acc[i] = added if first else acc[i] * shrink + added
+            acc[i, :, half] = added if first else acc[i, :, half] * shrink + added
 
     every = tuple(range(PIECES))
     half = PIECES // 2

time: 58.7 us -> 58.6 us (level)
  no operation moved by 1% of the time
where the time goes in v4:
time: 58.6 us; the launch traced here: 58.5 us
  Pallas kernels  56.6 us (97%)
  local copies, waits for them, and re-layouts  1.87 us (3%)
    pallas_call x1, Pallas kernels, body(): pl.pallas_call(functools.partial(kernel, n_seq, n_head), out_shape=jax.Sh...  56.6 us
    unnamed x1, local copies, waits for them, and re-layouts  1.87 us

profile of v4, /device:TPU:1, one launch (start us, length us, event | category | flops | bytes accessed | tf_op | source)
XLA Modules:
  0.0 58.5 jit_solution(4788782001789361630)
XLA Ops:
  0.0 56.6 %attend.1 = bf16[64,4096]{1,0:T(8,128)(2,1)} custom-call(bf16[512,512]{1,0:T(8,128)(2,1)} %q_hbm.1, bf16[512,128]{1,0:T(8,128)(2,1)} %k_hbm.1, bf16[512,128]{1,0:T(8,128)(2,1)} %v_hbm.1, s32[1,32]{1,0:T(1,128)} %bitcast.1), custom_call_target="tpu_custom_call" | custom-call | flops 4294967296 | bytes 2097152 | tf_op jit(solution)/shard_map/attend/pallas_call | solution.py:325
  56.6 1.9 %copy.6 = bf16[64,4096]{1,0:T(8,128)(2,1)} copy(bf16[64,4096]{1,0:T(8,128)(2,1)} %attend.1) | data formatting | bytes 1048576

commit v5 on v3

--- a/solution.py
+++ b/solution.py
@@ -17,7 +17,8 @@
 CORES = 2
 COLS = GROUP * B
 EXTRA = 16
-WINDOW = 2
+LAG_FORWARD = 2
+LAG_BACKWARD = 1
 
 NEG = -1e30
 SCALE = math.log2(math.e) / math.sqrt(HD)
@@ -41,13 +42,11 @@
     acc,
     reach,
     out_buf,
-    relay_buf,
     load_sem,
     send_sem,
     recv_sem,
     out_send,
     out_recv,
-    relay_sem,
 ):
     s = lax.axis_index("seq")
     h = lax.axis_index("head")
@@ -71,9 +70,6 @@
     loads.append(pltpu.make_async_copy(v_hbm, v_in, load_sem.at[PIECES]))
     loads.append(pltpu.make_async_copy(doc_hbm, doc_in, load_sem.at[PIECES + 1]))
     loads.append(pltpu.make_async_copy(q_hbm, q_in, load_sem.at[PIECES + 2]))
-    for copy in loads:
-        copy.start()
-
     barrier = pltpu.get_barrier_semaphore()
 
     def greet(to_seq, to_head):
@@ -84,6 +80,8 @@
     for step in range(1, n_head):
         greet(s, lax.rem(h + step, n_head))
 
+    for copy in loads:
+        copy.start()
     for copy in loads[: PIECES + 1]:
         copy.wait()
     for j in range(PIECES):
@@ -91,18 +89,18 @@
 
     pl.semaphore_wait(barrier, 6 + n_head - 1)
 
-    def move(src, dst, j, to):
+    def move(src, dst, j, to, lane=None):
         return pltpu.make_async_remote_copy(
             src_ref=kv.at[src, j],
             dst_ref=kv.at[dst, j],
-            send_sem=send_sem.at[dst, j],
+            send_sem=send_sem.at[dst if lane is None else lane, j],
             recv_sem=recv_sem.at[dst, j],
             device_id=(to, h),
             device_id_type=MESH,
         )
 
-    def send(src, dst, j, to):
-        move(src, dst, j, to).start()
+    def send(src, dst, j, to, lane=None):
+        move(src, dst, j, to, lane).start()
 
     def arrived(d, j):
         move(d, d, j, after).wait_recv()
@@ -111,9 +109,6 @@
         move(d, d, j, after).wait_send()
 
     whole = 3 * PIECES
-    longest = 4 * PIECES
-    forward_end = jnp.where(z == ROWS - 2, longest, whole)
-    backward_end = jnp.where(z == 0, whole, longest)
 
     def forward(n):
         return 1 + n // PIECES, lax.rem(n, PIECES)
@@ -121,7 +116,7 @@
     def backward(n):
         return FAR - 1 - n // PIECES, lax.rem(n, PIECES)
 
-    for j in range(WINDOW):
+    for j in range(PIECES):
         send(0, 1, j, after)
         send(0, FAR - 1, j, ahead)
 
@@ -201,63 +196,42 @@
         acc[i] = added if first else acc[i] * shrink + added
 
     every = tuple(range(PIECES))
-
-    late = PIECES - WINDOW
-    first_pair = PIECES + late - 1
-    steps = first_pair + whole
-    leaf_work = steps - PIECES
-    leaf = leaf_work - PIECES - 1
-
-    @pl.loop(0, steps)
+    half = PIECES // 2
+
+    first_pair = PIECES - 1 + LAG_FORWARD
+    leaf = first_pair
+    leaf_work = first_pair + PIECES + 1
+
+    @pl.loop(0, PIECES)
+    def _(i):
+        update(i, [(0, every)], first=True)
+
+    @pl.loop(0, first_pair + whole)
     def _(t):
-        n = t + WINDOW
-        here = t - late
-
-        @pl.when(t < forward_end)
-        def _():
-            sent(*forward(t))
-
-        @pl.when((here >= 0) & (here < whole))
-        def _():
-            arrived(*forward(here))
-
-        @pl.when(n < PIECES)
-        def _():
-            send(0, 1, n, after)
-
-        @pl.when((n >= PIECES) & (n < forward_end))
-        def _():
-            d, j = forward(n)
-            send(d - 1, d, j, after)
-
-        @pl.when(t < backward_end)
-        def _():
-            sent(*backward(t))
-
-        @pl.when((here >= 0) & (here < whole))
-        def _():
-            arrived(*backward(here))
-
-        @pl.when(n < PIECES)
-        def _():
-            send(0, FAR - 1, n, ahead)
-
-        @pl.when((n >= PIECES) & (n < backward_end))
-        def _():
-            d, j = backward(n)
-            send(d + 1, d, j, before)
-
-        @pl.when((t > leaf) & (t < leaf + PIECES - 1))
-        def _():
-            sent(FAR, t - leaf)
+        back = t - LAG_BACKWARD
+        ahead_n = t - LAG_FORWARD
+
+        @pl.when((back >= 0) & (back < whole))
+        def _():
+            d, j = backward(back)
+            arrived(d, j)
+
+            @pl.when((d > 5) | (z != 0))
+            def _():
+                send(d, d - 1, j, before)
+
+        @pl.when((ahead_n >= 0) & (ahead_n < whole))
+        def _():
+            d, j = forward(ahead_n)
+            arrived(d, j)
+
+            @pl.when((d < 3) | (z == ROWS - 2))
+            def _():
+                send(d, d + 1, j, after, lax.rem(d + 1, 4))
 
         @pl.when((t >= leaf) & (t < leaf + PIECES - 1))
         def _():
             send(0, FAR, t - leaf + 1, up)
-
-        @pl.when(t < PIECES)
-        def _():
-            update(t, [(0, every)], first=True)
 
         @pl.when(t >= first_pair)
         def _():
@@ -269,12 +243,18 @@
             for j in range(1, PIECES):
                 arrived(FAR, j)
 
-        @pl.when(t >= leaf_work)
+        @pl.when((t >= leaf_work) & (t < leaf_work + PIECES))
         def _():
             update(t - leaf_work, [(FAR, every[1:])])
 
-    sent(FAR, PIECES - 1)
-    for j in every:
+    for j in every[:half]:
+        arrived(4, j)
+
+    @pl.loop(0, PIECES)
+    def _(i):
+        update(i, [(4, every[:half])])
+
+    for j in every[half:]:
         arrived(4, j)
 
     def columns(who):
@@ -296,24 +276,12 @@
             device_id_type=MESH,
         )
 
-    relay_in = pltpu.make_async_remote_copy(
-        src_ref=out_buf.at[chip(2) * CORES + 1],
-        dst_ref=relay_buf,
-        send_sem=out_send.at[chip(2) * CORES + 1],
-        recv_sem=relay_sem.at[0],
-        device_id=(s, chip(1) * CORES + core_here),
-        device_id_type=MESH,
-    )
-    relay_out = deliver(
-        relay_buf, chip(chips - 1) * CORES + core_here, chip(1) * CORES + 1, relay_sem.at[1]
-    )
-
     for hop in (2, 1, 3, 0):
         i = chip(hop)
-        update(i, [(4, every)])
-        final = acc[i, :HD] * (1.0 / acc[i, HD : HD + 1])
+        update(i, [(4, every[half:])])
+        final = (acc[i, :HD] * (1.0 / acc[i, HD : HD + 1])).astype(jnp.bfloat16)
         for g in range(GROUP):
-            rows = final[:, g * B : (g + 1) * B].T.astype(jnp.bfloat16)
+            rows = final[:, g * B : (g + 1) * B].T
             for core in range(CORES):
                 part = B // CORES
                 out_buf[i * CORES + core, :, g * HD : (g + 1) * HD] = rows[
@@ -322,9 +290,7 @@
         for core in range(CORES):
             target = i * CORES + core
             there = deliver(out_buf.at[target], h, target, out_send.at[target])
-            if hop == 2 and core == 1:
-                relay_in.start()
-            elif hop:
+            if hop:
                 there.start()
             else:
 
@@ -336,15 +302,28 @@
                 def _():
                     own.start()
 
-    relay_in.wait_recv()
-    relay_out.start()
+    @pl.loop(0, PIECES)
+    def _(j):
+        for d in (1, 2, 3, 5, 6, 7):
+            sent(d, j)
+
+        @pl.when(z != 0)
+        def _():
+            sent(4, j)
+
+        @pl.when(z == ROWS - 2)
+        def _():
+            sent(0, j)
+
+        @pl.when(j > 0)
+        def _():
+            sent(FAR, j)
 
     for step in range(1, n_head):
         peer = lax.rem(h + step, n_head)
         other = deliver(out_buf.at[peer], peer, peer, out_send.at[peer])
         other.wait_send()
         other.wait_recv()
-    relay_out.wait_send()
     own.wait()
 
 
@@ -369,13 +348,11 @@
             pltpu.VMEM((PIECES, HD + EXTRA, COLS), f32),
             pltpu.VMEM((PIECES, 1, COLS), jnp.int32),
             pltpu.VMEM((n_head, part, COLS), bf16),
-            pltpu.VMEM((part, COLS), bf16),
             pltpu.SemaphoreType.DMA((PIECES + 3,)),
             pltpu.SemaphoreType.DMA((FAR + 1, PIECES)),
             pltpu.SemaphoreType.DMA((FAR + 1, PIECES)),
             pltpu.SemaphoreType.DMA((n_head,)),
             pltpu.SemaphoreType.DMA((n_head,)),
-            pltpu.SemaphoreType.DMA((2,)),
         ],
         compiler_params=pltpu.CompilerParams(
             collective_id=0, has_side_effects=True, vmem_limit_bytes=62 << 20

time: 60.7 us -> 61.3 us (level)
  Pallas kernels: 58.6 us -> 59.3 us
    pallas_call x1, Pallas kernels: 58.6 us -> 59.3 us  [body(): pl.pallas_call(functools.partial(kernel, n_seq, n_head), out_shape=jax.Sh...]
where the time goes in v5:
time: 61.3 us; the launch traced here: 61.2 us
  Pallas kernels  59.3 us (97%)
  local copies, waits for them, and re-layouts  1.87 us (3%)
    pallas_call x1, Pallas kernels, body(): pl.pallas_call(functools.partial(kernel, n_seq, n_head), out_shape=jax.Sh...  59.3 us
    unnamed x1, local copies, waits for them, and re-layouts  1.87 us

profile of v5, /device:TPU:1, one launch (start us, length us, event | category | flops | bytes accessed | tf_op | source)
XLA Modules:
  0.0 61.2 jit_solution(7650075378807162566)
XLA Ops:
  0.0 59.3 %attend.1 = bf16[64,4096]{1,0:T(8,128)(2,1)} custom-call(bf16[512,512]{1,0:T(8,128)(2,1)} %q_hbm.1, bf16[512,128]{1,0:T(8,128)(2,1)} %k_hbm.1, bf16[512,128]{1,0:T(8,128)(2,1)} %v_hbm.1, s32[1,32]{1,0:T(1,128)} %bitcast.1), custom_call_target="tpu_custom_call" | custom-call | flops 4294967296 | bytes 2097152 | tf_op jit(solution)/shard_map/attend/pallas_call | solution.py:336
  59.3 1.9 %copy.6 = bf16[64,4096]{1,0:T(8,128)(2,1)} copy(bf16[64,4096]{1,0:T(8,128)(2,1)} %attend.1) | data formatting | bytes 1048576

commit v6 on v1

--- a/solution.py
+++ b/solution.py
@@ -70,9 +70,6 @@
     loads.append(pltpu.make_async_copy(v_hbm, v_in, load_sem.at[PIECES]))
     loads.append(pltpu.make_async_copy(doc_hbm, doc_in, load_sem.at[PIECES + 1]))
     loads.append(pltpu.make_async_copy(q_hbm, q_in, load_sem.at[PIECES + 2]))
-    for copy in loads:
-        copy.start()
-
     barrier = pltpu.get_barrier_semaphore()
 
     def greet(to_seq, to_head):
@@ -91,6 +88,8 @@
     def _():
         greet(last_col, h)
 
+    for copy in loads:
+        copy.start()
     for copy in loads[: PIECES + 1]:
         copy.wait()
     for j in range(PIECES):
@@ -99,18 +98,18 @@
     edge = jnp.where((z == 0) | (z == ROWS - 1), 1, 0)
     pl.semaphore_wait(barrier, 4 + n_head - 1 + edge)
 
-    def move(src, dst, j, to):
+    def move(src, dst, j, to, lane=None):
         return pltpu.make_async_remote_copy(
             src_ref=kv.at[src, j],
             dst_ref=kv.at[dst, j],
-            send_sem=send_sem.at[dst, j],
+            send_sem=send_sem.at[dst if lane is None else lane, j],
             recv_sem=recv_sem.at[dst, j],
             device_id=(to, h),
             device_id_type=MESH,
         )
 
-    def send(src, dst, j, to):
-        move(src, dst, j, to).start()
+    def send(src, dst, j, to, lane=None):
+        move(src, dst, j, to, lane).start()
 
     def arrived(d, j):
         move(d, d, j, after).wait_recv()
@@ -225,6 +224,10 @@
             def _():
                 send(d, d - 1, j, before)
 
+            @pl.when((d == 5) & (z == 1))
+            def _():
+                send(5, 4, j, before, 0)
+
         u = t - LAG
         near = u // PIECES + 1
         k = lax.rem(u + PIECES, PIECES)
@@ -233,7 +236,7 @@
         def _():
             arrived(near, k)
 
-            @pl.when(near < 4)
+            @pl.when((near < 3) | ((near == 3) & (z != ROWS - 1)))
             def _():
                 send(near, near + 1, k, after)
 
@@ -260,9 +263,9 @@
         to_x = lax.rem(x + hop, chips)
         i = to_x
         update(i, [(5, every[half:]), (4, every[half:])])
-        final = acc[i, :HD] * (1.0 / acc[i, HD : HD + 1])
+        final = (acc[i, :HD] * (1.0 / acc[i, HD : HD + 1])).astype(jnp.bfloat16)
         for g in range(GROUP):
-            rows = final[:, g * B : (g + 1) * B].T.astype(jnp.bfloat16)
+            rows = final[:, g * B : (g + 1) * B].T
             for core in range(CORES):
                 part = B // CORES
                 out_buf[to_x * CORES + core, :, g * HD : (g + 1) * HD] = rows[
@@ -292,11 +295,18 @@
             else:
                 there.start()
 
-    @pl.loop(1, FAR + 1)
-    def _(d):
-        @pl.loop(0, PIECES)
-        def _(j):
+    @pl.loop(0, PIECES)
+    def _(j):
+        for d in (1, 2, 3, 5, 6, 7, 8):
             sent(d, j)
+
+        @pl.when(z != ROWS - 1)
+        def _():
+            sent(4, j)
+
+        @pl.when(z == 1)
+        def _():
+            sent(0, j)
 
     for step in range(1, n_head):
         peer = lax.rem(h + step, n_head)

time: 58.7 us -> 57.5 us (0.980)
  Pallas kernels: 56.6 us -> 55.5 us
    pallas_call x1, Pallas kernels: 56.6 us -> 55.5 us  [body(): pl.pallas_call(functools.partial(kernel, n_seq, n_head), out_shape=jax.Sh...]
where the time goes in v6:
time: 57.5 us; the launch traced here: 57.4 us
  Pallas kernels  55.5 us (97%)
  local copies, waits for them, and re-layouts  1.87 us (3%)
    pallas_call x1, Pallas kernels, body(): pl.pallas_call(functools.partial(kernel, n_seq, n_head), out_shape=jax.Sh...  55.5 us
    unnamed x1, local copies, waits for them, and re-layouts  1.87 us

profile of v6, /device:TPU:1, one launch (start us, length us, event | category | flops | bytes accessed | tf_op | source)
XLA Modules:
  0.0 57.4 jit_solution(2998418382736860114)
XLA Ops:
  0.0 55.5 %attend.1 = bf16[64,4096]{1,0:T(8,128)(2,1)} custom-call(bf16[512,512]{1,0:T(8,128)(2,1)} %q_hbm.1, bf16[512,128]{1,0:T(8,128)(2,1)} %k_hbm.1, bf16[512,128]{1,0:T(8,128)(2,1)} %v_hbm.1, s32[1,32]{1,0:T(1,128)} %bitcast.1), custom_call_target="tpu_custom_call" | custom-call | flops 4294967296 | bytes 2097152 | tf_op jit(solution)/shard_map/attend/pallas_call | solution.py:332
  55.5 1.9 %copy.6 = bf16[64,4096]{1,0:T(8,128)(2,1)} copy(bf16[64,4096]{1,0:T(8,128)(2,1)} %attend.1) | data formatting | bytes 1048576

commit v7 on v6

--- a/solution.py
+++ b/solution.py
@@ -18,6 +18,7 @@
 COLS = GROUP * B
 EXTRA = 16
 LAG = 2
+LAG_WRAP = 4
 
 NEG = -1e30
 SCALE = math.log2(math.e) / math.sqrt(HD)
@@ -61,6 +62,16 @@
     first_col = ring(-(ROWS - 1))
     last_col = ring(ROWS - 1)
 
+    def wanted(who, d):
+        beyond = d - who
+        return (beyond <= 0) | (beyond == ROWS - 2) | (beyond == ROWS - 1)
+
+    @pl.when(s < ROWS)
+    def _():
+        @pl.loop(1, FAR + 1)
+        def _(d):
+            kv[d] = jnp.zeros(kv.shape[1:], kv.dtype)
+
     loads = [
         pltpu.make_async_copy(
             k_hbm.at[pl.ds(j * B, B), :], kv.at[0, j, 0], load_sem.at[j]
@@ -109,13 +120,19 @@
         )
 
     def send(src, dst, j, to, lane=None):
-        move(src, dst, j, to, lane).start()
+        @pl.when(wanted(to, dst))
+        def _():
+            move(src, dst, j, to, lane).start()
 
     def arrived(d, j):
-        move(d, d, j, after).wait_recv()
-
-    def sent(d, j):
-        move(d, d, j, after).wait_send()
+        @pl.when(wanted(s, d))
+        def _():
+            move(d, d, j, after).wait_recv()
+
+    def sent(d, j, to, lane=None):
+        @pl.when(wanted(to, d))
+        def _():
+            move(d, d, j, to, lane).wait_send()
 
     for j in range(PIECES):
         send(0, FAR, j, up)
@@ -209,9 +226,10 @@
         update(j, [(0, every)], first=True)
 
     far_steps = 4 * PIECES
-    work_from = PIECES - 1 + LAG
-
-    @pl.loop(0, 3 * PIECES + work_from)
+    lag = jnp.where(z < 2, LAG_WRAP, LAG)
+    work_from = PIECES - 1 + lag
+
+    @pl.loop(0, 4 * PIECES - 1 + LAG_WRAP)
     def _(t):
         j = lax.rem(t, PIECES)
         d = FAR - t // PIECES
@@ -228,11 +246,11 @@
             def _():
                 send(5, 4, j, before, 0)
 
-        u = t - LAG
+        u = t - lag
         near = u // PIECES + 1
         k = lax.rem(u + PIECES, PIECES)
 
-        @pl.when(u >= 0)
+        @pl.when((u >= 0) & (u < 4 * PIECES - 1))
         def _():
             arrived(near, k)
 
@@ -242,7 +260,7 @@
 
         w = t - work_from
 
-        @pl.when(w >= 0)
+        @pl.when((w >= 0) & (w < 3 * PIECES))
         def _():
             p = w // PIECES + 1
             update(lax.rem(w, PIECES), [(p, every), (FAR + 1 - p, every)])
@@ -251,8 +269,7 @@
     def _(j):
         update(j, [(5, every[:half]), (4, every[:half])])
 
-    for u in range(3 * PIECES + work_from - LAG, 4 * PIECES):
-        arrived(u // PIECES + 1, u % PIECES)
+    arrived(4, PIECES - 1)
 
     own = pltpu.make_async_copy(
         out_buf.at[h],
@@ -297,16 +314,20 @@
 
     @pl.loop(0, PIECES)
     def _(j):
-        for d in (1, 2, 3, 5, 6, 7, 8):
-            sent(d, j)
+        for d in (1, 2, 3):
+            sent(d, j, after)
+        for d in (5, 6):
+            sent(d, j, before)
+        sent(7, j, jnp.where(z == 0, last_col, before))
+        sent(FAR, j, up)
 
         @pl.when(z != ROWS - 1)
         def _():
-            sent(4, j)
+            sent(4, j, after)
 
         @pl.when(z == 1)
         def _():
-            sent(0, j)
+            sent(4, j, before, 0)
 
     for step in range(1, n_head):
         peer = lax.rem(h + step, n_head)

time: 57.5 us -> 54.9 us (0.955)
  the two profiles are of different devices: /device:TPU:1 before, /device:TPU:9 now
where the time goes in v7:
time: 54.9 us; the launch traced here: 54.7 us
  Pallas kernels  52.8 us (96%)
  local copies, waits for them, and re-layouts  1.87 us (3%)
    pallas_call x1, Pallas kernels, body(): pl.pallas_call(functools.partial(kernel, n_seq, n_head), out_shape=jax.Sh...  52.8 us
    unnamed x1, local copies, waits for them, and re-layouts  1.87 us

profile of v7, /device:TPU:9, one launch (start us, length us, event | category | flops | bytes accessed | tf_op | source)
XLA Modules:
  0.0 54.7 jit_solution(6122166613195037671)
XLA Ops:
  0.0 52.8 %attend.1 = bf16[64,4096]{1,0:T(8,128)(2,1)} custom-call(bf16[512,512]{1,0:T(8,128)(2,1)} %q_hbm.1, bf16[512,128]{1,0:T(8,128)(2,1)} %k_hbm.1, bf16[512,128]{1,0:T(8,128)(2,1)} %v_hbm.1, s32[1,32]{1,0:T(1,128)} %bitcast.1), custom_call_target="tpu_custom_call" | custom-call | flops 4294967296 | bytes 2097152 | tf_op jit(solution)/shard_map/attend/pallas_call | solution.py:353
  52.9 1.9 %copy.6 = bf16[64,4096]{1,0:T(8,128)(2,1)} copy(bf16[64,4096]{1,0:T(8,128)(2,1)} %attend.1) | data formatting | bytes 1048576

commit v8 on v7

--- a/solution.py
+++ b/solution.py
@@ -17,6 +17,7 @@
 CORES = 2
 COLS = GROUP * B
 EXTRA = 16
+WINDOW = 2
 LAG = 2
 LAG_WRAP = 4
 
@@ -135,7 +136,11 @@
             move(d, d, j, to, lane).wait_send()
 
     for j in range(PIECES):
-        send(0, FAR, j, up)
+        if j < WINDOW:
+
+            @pl.when(z != 0)
+            def _():
+                send(0, FAR, j, up)
 
         send(0, 1, j, after)
 
@@ -222,23 +227,27 @@
     half = PIECES // 2
 
     @pl.loop(0, PIECES)
-    def _(j):
-        update(j, [(0, every)], first=True)
-
-    far_steps = 4 * PIECES
+    def _(i):
+        update(i, [(0, every)], first=True)
+
+        @pl.when((z != 0) & (i < PIECES - WINDOW))
+        def _():
+            sent(FAR, i, up)
+            send(0, FAR, i + WINDOW, up)
+
     lag = jnp.where(z < 2, LAG_WRAP, LAG)
-    work_from = PIECES - 1 + lag
-
-    @pl.loop(0, 4 * PIECES - 1 + LAG_WRAP)
+    work_from = 2 * PIECES - 1
+
+    @pl.loop(0, 3 * PIECES + work_from)
     def _(t):
         j = lax.rem(t, PIECES)
         d = FAR - t // PIECES
 
-        @pl.when(t < far_steps)
+        @pl.when((t < 4 * PIECES) & ((d < FAR) | (z != 0)))
         def _():
             arrived(d, j)
 
-            @pl.when((d > 5) & ((d < FAR) | (z != 0)))
+            @pl.when(d > 5)
             def _():
                 send(d, d - 1, j, before)
 
@@ -246,30 +255,44 @@
             def _():
                 send(5, 4, j, before, 0)
 
+        @pl.when((z == 0) & (t > PIECES) & (t < 2 * PIECES))
+        def _():
+            send(0, FAR, j, up)
+
         u = t - lag
         near = u // PIECES + 1
         k = lax.rem(u + PIECES, PIECES)
 
-        @pl.when((u >= 0) & (u < 4 * PIECES - 1))
+        @pl.when((u >= 0) & (u < 3 * PIECES))
         def _():
             arrived(near, k)
 
-            @pl.when((near < 3) | ((near == 3) & (z != ROWS - 1)))
+            @pl.when((near < 3) | (z != ROWS - 1))
             def _():
                 send(near, near + 1, k, after)
 
         w = t - work_from
 
-        @pl.when((w >= 0) & (w < 3 * PIECES))
+        @pl.when(w >= 0)
         def _():
             p = w // PIECES + 1
-            update(lax.rem(w, PIECES), [(p, every), (FAR + 1 - p, every)])
+            update(lax.rem(w, PIECES), [(p, every), (FAR - p, every)])
+
+    for j in every[1:]:
+
+        @pl.when(z == 0)
+        def _():
+            arrived(FAR, j)
+
+    for j in every[:half]:
+        arrived(4, j)
 
     @pl.loop(0, PIECES)
-    def _(j):
-        update(j, [(5, every[:half]), (4, every[:half])])
-
-    arrived(4, PIECES - 1)
+    def _(i):
+        update(i, [(FAR, every[1:]), (4, every[:half])])
+
+    for j in every[half:]:
+        arrived(4, j)
 
     own = pltpu.make_async_copy(
         out_buf.at[h],
@@ -279,7 +302,7 @@
     for hop in (2, 1, 3, 0):
         to_x = lax.rem(x + hop, chips)
         i = to_x
-        update(i, [(5, every[half:]), (4, every[half:])])
+        update(i, [(4, every[half:])])
         final = (acc[i, :HD] * (1.0 / acc[i, HD : HD + 1])).astype(jnp.bfloat16)
         for g in range(GROUP):
             rows = final[:, g * B : (g + 1) * B].T
@@ -319,7 +342,10 @@
         for d in (5, 6):
             sent(d, j, before)
         sent(7, j, jnp.where(z == 0, last_col, before))
-        sent(FAR, j, up)
+
+        @pl.when(jnp.where(z == 0, j > 0, j >= PIECES - WINDOW))
+        def _():
+            sent(FAR, j, up)
 
         @pl.when(z != ROWS - 1)
         def _():

time: 54.9 us -> 55.9 us (1.018)
  the two profiles are of different devices: /device:TPU:9 before, /device:TPU:49 now
where the time goes in v8:
time: 55.9 us; the launch traced here: 55.7 us
  Pallas kernels  53.8 us (96%)
  local copies, waits for them, and re-layouts  1.87 us (3%)
    pallas_call x1, Pallas kernels, body(): pl.pallas_call(functools.partial(kernel, n_seq, n_head), out_shape=jax.Sh...  53.8 us
    unnamed x1, local copies, waits for them, and re-layouts  1.87 us

profile of v8, /device:TPU:49, one launch (start us, length us, event | category | flops | bytes accessed | tf_op | source)
XLA Modules:
  0.0 55.7 jit_solution(17777486423936031701)
XLA Ops:
  0.0 53.8 %attend.1 = bf16[64,4096]{1,0:T(8,128)(2,1)} custom-call(bf16[512,512]{1,0:T(8,128)(2,1)} %q_hbm.1, bf16[512,128]{1,0:T(8,128)(2,1)} %k_hbm.1, bf16[512,128]{1,0:T(8,128)(2,1)} %v_hbm.1, s32[1,32]{1,0:T(1,128)} %bitcast.1), custom_call_target="tpu_custom_call" | custom-call | flops 4294967296 | bytes 2097152 | tf_op jit(solution)/shard_map/attend/pallas_call | solution.py:379
  53.8 1.9 %copy.6 = bf16[64,4096]{1,0:T(8,128)(2,1)} copy(bf16[64,4096]{1,0:T(8,128)(2,1)} %attend.1) | data formatting | bytes 1048576

commit v9 on v7

--- a/solution.py
+++ b/solution.py
@@ -169,61 +169,63 @@
             q_t[i, :HD, g * B : (g + 1) * B] = high
             q_t[i, HD:, g * B : (g + 1) * B] = (scaled - high.astype(jnp.float32)).astype(jnp.bfloat16)
 
-    def update(i, chunks, first=False):
-        queries = q_t[i]
-        far = reach[i]
-        scores, shown = [], []
+    def update(which, chunks, first=False):
+        ones = jnp.ones((EXTRA, B), jnp.bfloat16)
+        keys, values, pairs = [], [], []
         for d, blocks in chunks:
             n = len(blocks)
-            keys = kv[d, blocks[0] : blocks[0] + n, 0].reshape(n * B, HD)
-            pair = jnp.dot(
-                jnp.concatenate([keys, keys], axis=1), queries, preferred_element_type=jnp.float32
-            )
-            for b, j in enumerate(blocks):
-                block = pair[b * B : (b + 1) * B]
+            part = kv[d, blocks[0] : blocks[0] + n, 0].reshape(n * B, HD)
+            keys.append(jnp.concatenate([part, part], axis=1))
+            values += [jnp.concatenate([kv[d, j, 1], ones], axis=0) for j in blocks]
+            pairs += [(d, j) for j in blocks]
+        keys = jnp.concatenate(keys, axis=0)
+        values = jnp.concatenate(values, axis=1)
+        queries = [q_t[i] for i in which]
+        reaches = [reach[i] for i in which]
+        if not first:
+            peaks = [top[i] for i in which]
+            sums = [acc[i] for i in which]
+        products = [jnp.dot(keys, q, preferred_element_type=jnp.float32) for q in queries]
+        results = []
+        for n, (i, far, product) in enumerate(zip(which, reaches, products)):
+            scores, shown = [], []
+            for b, (d, j) in enumerate(pairs):
+                block = product[b * B : (b + 1) * B]
                 delta = PIECES * d + i - j
+                show = delta <= far
                 if first:
                     key = lax.broadcasted_iota(jnp.int32, (B, COLS), 0) + j * B
                     query = lax.rem(lax.broadcasted_iota(jnp.int32, (B, COLS), 1), B) + i * B
                     block = jnp.where(key <= query, block, NEG)
-                    shown.append((delta <= far) & (delta >= 0))
-                else:
-                    shown.append(delta <= far)
+                    show = show & (delta >= 0)
+                shown.append(show)
                 scores.append(block)
-        peak = None
-        for block, show in zip(scores, shown):
-            here = jnp.where(show, jnp.max(block, axis=0, keepdims=True), NEG)
-            peak = here if peak is None else jnp.maximum(peak, here)
-        if not first:
-            old = top[i]
-            peak = jnp.maximum(old, peak)
-            shrink = jnp.exp2(old - peak)
-        top[i] = peak
-        added = None
-        at = 0
-        ones = jnp.ones((EXTRA, B), jnp.bfloat16)
-        for d, blocks in chunks:
-            n = len(blocks)
+            peak = None
+            for block, show in zip(scores, shown):
+                here = jnp.where(show, jnp.max(block, axis=0, keepdims=True), NEG)
+                peak = here if peak is None else jnp.maximum(peak, here)
+            if not first:
+                peak = jnp.maximum(peaks[n], peak)
+                shrink = jnp.exp2(peaks[n] - peak)
             weights = [
                 jnp.exp2(block - jnp.where(show, peak, -NEG)).astype(jnp.bfloat16)
-                for block, show in zip(scores[at : at + n], shown[at : at + n])
+                for block, show in zip(scores, shown)
             ]
-            at += n
-            values = jnp.concatenate(
-                [jnp.concatenate([kv[d, j, 1], ones], axis=0) for j in blocks], axis=1
-            )
-            part = jnp.dot(
+            added = jnp.dot(
                 values, jnp.concatenate(weights, axis=0), preferred_element_type=jnp.float32
             )
-            added = part if added is None else added + part
-        acc[i] = added if first else acc[i] * shrink + added
+            results.append((peak, added if first else sums[n] * shrink + added))
+        for i, (peak, total) in zip(which, results):
+            top[i] = peak
+            acc[i] = total
+        return [total for _, total in results]
 
     every = tuple(range(PIECES))
     half = PIECES // 2
 
-    @pl.loop(0, PIECES)
-    def _(j):
-        update(j, [(0, every)], first=True)
+    @pl.loop(0, PIECES // 2)
+    def _(i):
+        update((2 * i, 2 * i + 1), [(0, every)], first=True)
 
     far_steps = 4 * PIECES
     lag = jnp.where(z < 2, LAG_WRAP, LAG)
@@ -263,11 +265,13 @@
         @pl.when((w >= 0) & (w < 3 * PIECES))
         def _():
             p = w // PIECES + 1
-            update(lax.rem(w, PIECES), [(p, every), (FAR + 1 - p, every)])
-
-    @pl.loop(0, PIECES)
-    def _(j):
-        update(j, [(5, every[:half]), (4, every[:half])])
+            i = 2 * lax.rem(w, 2)
+            chunk = jnp.where(lax.rem(w, PIECES) < 2, FAR + 1 - p, p)
+            update((i, i + 1), [(chunk, every)])
+
+    @pl.loop(0, PIECES // 2)
+    def _(i):
+        update((2 * i, 2 * i + 1), [(5, every[:half]), (4, every[:half])])
 
     arrived(4, PIECES - 1)
 
@@ -276,41 +280,39 @@
         out_ref.at[:, pl.ds(pl.multiple_of(h * COLS, COLS), COLS)],
         load_sem.at[0],
     )
-    for hop in (2, 1, 3, 0):
-        to_x = lax.rem(x + hop, chips)
-        i = to_x
-        update(i, [(5, every[half:]), (4, every[half:])])
-        final = (acc[i, :HD] * (1.0 / acc[i, HD : HD + 1])).astype(jnp.bfloat16)
-        for g in range(GROUP):
-            rows = final[:, g * B : (g + 1) * B].T
+    for hops in ((2, 1), (3, 0)):
+        which = [lax.rem(x + hop, chips) for hop in hops]
+        totals = update(which, [(5, every[half:]), (4, every[half:])])
+        for hop, i, total in zip(hops, which, totals):
+            final = (total[:HD] * (1.0 / total[HD : HD + 1])).astype(jnp.bfloat16)
+            part = B // CORES
+            for g in range(GROUP):
+                rows = final[:, g * B : (g + 1) * B].T
+                for core in range(CORES):
+                    out_buf[i * CORES + core, :, g * HD : (g + 1) * HD] = rows[
+                        core * part : (core + 1) * part
+                    ]
             for core in range(CORES):
-                part = B // CORES
-                out_buf[to_x * CORES + core, :, g * HD : (g + 1) * HD] = rows[
-                    core * part : (core + 1) * part
-                ]
-        for core in range(CORES):
-            target = to_x * CORES + core
-            step = lax.rem(target - h + n_head, n_head)
-            there = pltpu.make_async_remote_copy(
-                src_ref=out_buf.at[target],
-                dst_ref=out_ref.at[:, pl.ds(pl.multiple_of(h * COLS, COLS), COLS)],
-                send_sem=out_send.at[target],
-                recv_sem=out_recv.at[h],
-                device_id=(s, target),
-                device_id_type=MESH,
-            )
-            if hop == 0:
-
-                @pl.when(step != 0)
-                def _():
+                target = i * CORES + core
+                there = pltpu.make_async_remote_copy(
+                    src_ref=out_buf.at[target],
+                    dst_ref=out_ref.at[:, pl.ds(pl.multiple_of(h * COLS, COLS), COLS)],
+                    send_sem=out_send.at[target],
+                    recv_sem=out_recv.at[h],
+                    device_id=(s, target),
+                    device_id_type=MESH,
+                )
+                if hop:
                     there.start()
-
-                @pl.when(step == 0)
-                def _():
-                    own.start()
-
-            else:
-                there.start()
+                else:
+
+                    @pl.when(h != target)
+                    def _():
+                        there.start()
+
+                    @pl.when(h == target)
+                    def _():
+                        own.start()
 
     @pl.loop(0, PIECES)
     def _(j):

time: 54.9 us -> 53.6 us (0.976)
  the two profiles are of different devices: /device:TPU:9 before, /device:TPU:49 now
where the time goes in v9:
time: 53.6 us; the launch traced here: 53.4 us
  Pallas kernels  51.5 us (96%)
  local copies, waits for them, and re-layouts  1.87 us (3%)
    pallas_call x1, Pallas kernels, body(): pl.pallas_call(functools.partial(kernel, n_seq, n_head), out_shape=jax.Sh...  51.5 us
    unnamed x1, local copies, waits for them, and re-layouts  1.87 us

profile of v9, /device:TPU:49, one launch (start us, length us, event | category | flops | bytes accessed | tf_op | source)
XLA Modules:
  0.0 53.4 jit_solution(15610980212610101676)
XLA Ops:
  0.0 51.5 %attend.1 = bf16[64,4096]{1,0:T(8,128)(2,1)} custom-call(bf16[512,512]{1,0:T(8,128)(2,1)} %q_hbm.1, bf16[512,128]{1,0:T(8,128)(2,1)} %k_hbm.1, bf16[512,128]{1,0:T(8,128)(2,1)} %v_hbm.1, s32[1,32]{1,0:T(1,128)} %bitcast.1), custom_call_target="tpu_custom_call" | custom-call | flops 4294967296 | bytes 2097152 | tf_op jit(solution)/shard_map/attend/pallas_call | solution.py:355
  51.5 1.9 %copy.6 = bf16[64,4096]{1,0:T(8,128)(2,1)} copy(bf16[64,4096]{1,0:T(8,128)(2,1)} %attend.1) | data formatting | bytes 1048576

commit v10 on v9

--- a/solution.py
+++ b/solution.py
@@ -229,18 +229,18 @@
 
     far_steps = 4 * PIECES
     lag = jnp.where(z < 2, LAG_WRAP, LAG)
-    work_from = PIECES - 1 + lag
-
-    @pl.loop(0, 4 * PIECES - 1 + LAG_WRAP)
+    work_from = lag + 1
+
+    @pl.loop(0, 3 * PIECES + 1 + LAG_WRAP)
     def _(t):
         j = lax.rem(t, PIECES)
         d = FAR - t // PIECES
 
-        @pl.when(t < far_steps)
+        @pl.when((t < far_steps) & ((d < FAR) | (z != 0)))
         def _():
             arrived(d, j)
 
-            @pl.when((d > 5) & ((d < FAR) | (z != 0)))
+            @pl.when(d > 5)
             def _():
                 send(d, d - 1, j, before)
 
@@ -248,15 +248,20 @@
             def _():
                 send(5, 4, j, before, 0)
 
+        @pl.when((z == 0) & (t == work_from))
+        def _():
+            for k in range(PIECES):
+                arrived(FAR, k)
+
         u = t - lag
         near = u // PIECES + 1
         k = lax.rem(u + PIECES, PIECES)
 
-        @pl.when((u >= 0) & (u < 4 * PIECES - 1))
+        @pl.when((u >= 0) & (u < 3 * PIECES))
         def _():
             arrived(near, k)
 
-            @pl.when((near < 3) | ((near == 3) & (z != ROWS - 1)))
+            @pl.when((near < 3) | (z != ROWS - 1))
             def _():
                 send(near, near + 1, k, after)
 
@@ -271,9 +276,17 @@
 
     @pl.loop(0, PIECES // 2)
     def _(i):
-        update((2 * i, 2 * i + 1), [(5, every[:half]), (4, every[:half])])
-
-    arrived(4, PIECES - 1)
+        update((2 * i, 2 * i + 1), [(5, every)])
+
+    for j in every[:half]:
+        arrived(4, j)
+
+    @pl.loop(0, PIECES // 2)
+    def _(i):
+        update((2 * i, 2 * i + 1), [(4, every[:half])])
+
+    for j in every[half:]:
+        arrived(4, j)
 
     own = pltpu.make_async_copy(
         out_buf.at[h],
@@ -282,7 +295,7 @@
     )
     for hops in ((2, 1), (3, 0)):
         which = [lax.rem(x + hop, chips) for hop in hops]
-        totals = update(which, [(5, every[half:]), (4, every[half:])])
+        totals = update(which, [(4, every[half:])])
         for hop, i, total in zip(hops, which, totals):
             final = (total[:HD] * (1.0 / total[HD : HD + 1])).astype(jnp.bfloat16)
             part = B // CORES

time: 53.6 us -> 52.6 us (0.981)
  Pallas kernels: 51.5 us -> 50.6 us
    pallas_call x1, Pallas kernels: 51.5 us -> 50.6 us  [body(): pl.pallas_call(functools.partial(kernel, n_seq, n_head), out_shape=jax.Sh...]
where the time goes in v10:
time: 52.6 us; the launch traced here: 52.5 us
  Pallas kernels  50.6 us (96%)
  local copies, waits for them, and re-layouts  1.87 us (4%)
    pallas_call x1, Pallas kernels, body(): pl.pallas_call(functools.partial(kernel, n_seq, n_head), out_shape=jax.Sh...  50.6 us
    unnamed x1, local copies, waits for them, and re-layouts  1.87 us

profile of v10, /device:TPU:49, one launch (start us, length us, event | category | flops | bytes accessed | tf_op | source)
XLA Modules:
  0.0 52.5 jit_solution(6364700319742732840)
XLA Ops:
  0.0 50.6 %attend.1 = bf16[64,4096]{1,0:T(8,128)(2,1)} custom-call(bf16[512,512]{1,0:T(8,128)(2,1)} %q_hbm.1, bf16[512,128]{1,0:T(8,128)(2,1)} %k_hbm.1, bf16[512,128]{1,0:T(8,128)(2,1)} %v_hbm.1, s32[1,32]{1,0:T(1,128)} %bitcast.1), custom_call_target="tpu_custom_call" | custom-call | flops 4294967296 | bytes 2097152 | tf_op jit(solution)/shard_map/attend/pallas_call | solution.py:368
  50.6 1.9 %copy.6 = bf16[64,4096]{1,0:T(8,128)(2,1)} copy(bf16[64,4096]{1,0:T(8,128)(2,1)} %attend.1) | data formatting | bytes 1048576

commit v11 on v10

--- a/solution.py
+++ b/solution.py
@@ -17,6 +17,7 @@
 CORES = 2
 COLS = GROUP * B
 EXTRA = 16
+WINDOW = PIECES // 2
 LAG = 2
 LAG_WRAP = 4
 
@@ -135,7 +136,13 @@
             move(d, d, j, to, lane).wait_send()
 
     for j in range(PIECES):
-        send(0, FAR, j, up)
+        if j < WINDOW:
+            send(0, FAR, j, up)
+        else:
+
+            @pl.when(z == 0)
+            def _():
+                send(0, FAR, j, up)
 
         send(0, 1, j, after)
 
@@ -227,6 +234,11 @@
     def _(i):
         update((2 * i, 2 * i + 1), [(0, every)], first=True)
 
+        @pl.when(z != 0)
+        def _():
+            sent(FAR, i, up)
+            send(0, FAR, i + WINDOW, up)
+
     far_steps = 4 * PIECES
     lag = jnp.where(z < 2, LAG_WRAP, LAG)
     work_from = lag + 1
@@ -334,7 +346,10 @@
         for d in (5, 6):
             sent(d, j, before)
         sent(7, j, jnp.where(z == 0, last_col, before))
-        sent(FAR, j, up)
+
+        @pl.when((z == 0) | (j >= PIECES - WINDOW))
+        def _():
+            sent(FAR, j, up)
 
         @pl.when(z != ROWS - 1)
         def _():

time: 52.6 us -> 53.5 us (1.017)
  Pallas kernels: 50.6 us -> 51.5 us
    pallas_call x1, Pallas kernels: 50.6 us -> 51.5 us  [body(): pl.pallas_call(functools.partial(kernel, n_seq, n_head), out_shape=jax.Sh...]
where the time goes in v11:
time: 53.5 us; the launch traced here: 53.3 us
  Pallas kernels  51.5 us (96%)
  local copies, waits for them, and re-layouts  1.87 us (3%)
    pallas_call x1, Pallas kernels, body(): pl.pallas_call(functools.partial(kernel, n_seq, n_head), out_shape=jax.Sh...  51.5 us
    unnamed x1, local copies, waits for them, and re-layouts  1.87 us

profile of v11, /device:TPU:49, one launch (start us, length us, event | category | flops | bytes accessed | tf_op | source)
XLA Modules:
  0.0 53.3 jit_solution(5573950050321720446)
XLA Ops:
  0.0 51.5 %attend.1 = bf16[64,4096]{1,0:T(8,128)(2,1)} custom-call(bf16[512,512]{1,0:T(8,128)(2,1)} %q_hbm.1, bf16[512,128]{1,0:T(8,128)(2,1)} %k_hbm.1, bf16[512,128]{1,0:T(8,128)(2,1)} %v_hbm.1, s32[1,32]{1,0:T(1,128)} %bitcast.1), custom_call_target="tpu_custom_call" | custom-call | flops 4294967296 | bytes 2097152 | tf_op jit(solution)/shard_map/attend/pallas_call | solution.py:383
  51.5 1.9 %copy.6 = bf16[64,4096]{1,0:T(8,128)(2,1)} copy(bf16[64,4096]{1,0:T(8,128)(2,1)} %attend.1) | data formatting | bytes 1048576

commit v12 on v10

--- a/solution.py
+++ b/solution.py
@@ -244,7 +244,7 @@
             def _():
                 send(d, d - 1, j, before)
 
-            @pl.when((d == 5) & (z == 1))
+            @pl.when((d == 5) & (z == 1) & (j >= half))
             def _():
                 send(5, 4, j, before, 0)
 
@@ -261,7 +261,7 @@
         def _():
             arrived(near, k)
 
-            @pl.when((near < 3) | (z != ROWS - 1))
+            @pl.when((near < 3) | (z != ROWS - 1) | (k < half))
             def _():
                 send(near, near + 1, k, after)
 
@@ -336,11 +336,11 @@
         sent(7, j, jnp.where(z == 0, last_col, before))
         sent(FAR, j, up)
 
-        @pl.when(z != ROWS - 1)
+        @pl.when((z != ROWS - 1) | (j < half))
         def _():
             sent(4, j, after)
 
-        @pl.when(z == 1)
+        @pl.when((z == 1) & (j >= half))
         def _():
             sent(4, j, before, 0)
 

time: 52.6 us -> 52.7 us (level)
  the two profiles are of different devices: /device:TPU:49 before, /device:TPU:9 now
where the time goes in v12:
time: 52.7 us; the launch traced here: 52.5 us
  Pallas kernels  50.6 us (96%)
  local copies, waits for them, and re-layouts  1.87 us (4%)
    pallas_call x1, Pallas kernels, body(): pl.pallas_call(functools.partial(kernel, n_seq, n_head), out_shape=jax.Sh...  50.6 us
    unnamed x1, local copies, waits for them, and re-layouts  1.87 us

profile of v12, /device:TPU:9, one launch (start us, length us, event | category | flops | bytes accessed | tf_op | source)
XLA Modules:
  0.0 52.5 jit_solution(736271282645039616)
XLA Ops:
  0.0 50.6 %attend.1 = bf16[64,4096]{1,0:T(8,128)(2,1)} custom-call(bf16[512,512]{1,0:T(8,128)(2,1)} %q_hbm.1, bf16[512,128]{1,0:T(8,128)(2,1)} %k_hbm.1, bf16[512,128]{1,0:T(8,128)(2,1)} %v_hbm.1, s32[1,32]{1,0:T(1,128)} %bitcast.1), custom_call_target="tpu_custom_call" | custom-call | flops 4294967296 | bytes 2097152 | tf_op jit(solution)/shard_map/attend/pallas_call | solution.py:368
  50.7 1.9 %copy.6 = bf16[64,4096]{1,0:T(8,128)(2,1)} copy(bf16[64,4096]{1,0:T(8,128)(2,1)} %attend.1) | data formatting | bytes 1048576

commit v13 on v10

--- a/solution.py
+++ b/solution.py
@@ -18,7 +18,7 @@
 COLS = GROUP * B
 EXTRA = 16
 LAG = 2
-LAG_WRAP = 4
+LAG_WRAP = 3
 
 NEG = -1e30
 SCALE = math.log2(math.e) / math.sqrt(HD)
@@ -72,15 +72,13 @@
         def _(d):
             kv[d] = jnp.zeros(kv.shape[1:], kv.dtype)
 
-    loads = [
-        pltpu.make_async_copy(
-            k_hbm.at[pl.ds(j * B, B), :], kv.at[0, j, 0], load_sem.at[j]
-        )
-        for j in range(PIECES)
-    ]
-    loads.append(pltpu.make_async_copy(v_hbm, v_in, load_sem.at[PIECES]))
-    loads.append(pltpu.make_async_copy(doc_hbm, doc_in, load_sem.at[PIECES + 1]))
-    loads.append(pltpu.make_async_copy(q_hbm, q_in, load_sem.at[PIECES + 2]))
+    load_keys = pltpu.make_async_copy(k_hbm, kv.at[0, :, 0], load_sem.at[0])
+    load_values = pltpu.make_async_copy(v_hbm, v_in, load_sem.at[1])
+    load_lengths = pltpu.make_async_copy(doc_hbm, doc_in, load_sem.at[2])
+    load_queries = pltpu.make_async_copy(q_hbm, q_in, load_sem.at[3])
+    load_values.start()
+    load_keys.start()
+
     barrier = pltpu.get_barrier_semaphore()
 
     def greet(to_seq, to_head):
@@ -88,9 +86,6 @@
 
     for to in (after, before, up, down):
         greet(to, h)
-    for step in range(1, n_head):
-        greet(s, lax.rem(h + step, n_head))
-
     @pl.when(z == ROWS - 1)
     def _():
         greet(first_col, h)
@@ -99,12 +94,15 @@
     def _():
         greet(last_col, h)
 
-    for copy in loads:
-        copy.start()
-    for copy in loads[: PIECES + 1]:
-        copy.wait()
+    for step in range(1, n_head):
+        greet(s, lax.rem(h + step, n_head))
+
+    load_queries.start()
+    load_lengths.start()
+    load_values.wait()
     for j in range(PIECES):
         kv[0, j, 1] = v_in[pl.ds(j * B, B), :].T
+    load_keys.wait()
 
     edge = jnp.where((z == 0) | (z == ROWS - 1), 1, 0)
     pl.semaphore_wait(barrier, 4 + n_head - 1 + edge)
@@ -143,7 +141,7 @@
         def _():
             send(0, FAR - 1, j, last_col)
 
-    loads[PIECES + 1].wait()
+    load_lengths.wait()
     lengths = doc_in[...]
     count = lengths.shape[1]
     shape = (count, count)
@@ -160,7 +158,7 @@
         ).astype(jnp.int32)
         reach[i] = jnp.broadcast_to(block - start, (1, COLS))
 
-    loads[PIECES + 2].wait()
+    load_queries.wait()
     for i in range(PIECES):
         for g in range(GROUP):
             rows = q_in[i * B : (i + 1) * B, g * HD : (g + 1) * HD]
@@ -380,7 +378,7 @@
             pltpu.VMEM((PIECES, HD + EXTRA, COLS), f32),
             pltpu.VMEM((PIECES, 1, COLS), jnp.int32),
             pltpu.VMEM((n_head, part, COLS), bf16),
-            pltpu.SemaphoreType.DMA((PIECES + 3,)),
+            pltpu.SemaphoreType.DMA((4,)),
             pltpu.SemaphoreType.DMA((FAR + 1, PIECES)),
             pltpu.SemaphoreType.DMA((FAR + 1, PIECES)),
             pltpu.SemaphoreType.DMA((n_head,)),
@@ -393,7 +391,7 @@
             flops=4 * pairs * HD, bytes_accessed=2 << 20, transcendentals=pairs
         ),
         name="attend",
-    )(queries, key_rows, value_rows, doc_blocks.reshape(1, -1))
+    )(queries, key_rows.reshape(PIECES, B, HD), value_rows, doc_blocks.reshape(1, -1))
 
 
 def solution(mesh):

time: 52.6 us -> 52.6 us (level)
  no operation moved by 1% of the time
where the time goes in v13:
time: 52.6 us; the launch traced here: 52.5 us
  Pallas kernels  50.6 us (96%)
  local copies, waits for them, and re-layouts  1.87 us (4%)
    pallas_call x1, Pallas kernels, body(): pl.pallas_call(functools.partial(kernel, n_seq, n_head), out_shape=jax.Sh...  50.6 us
    unnamed x1, local copies, waits for them, and re-layouts  1.87 us

profile of v13, /device:TPU:49, one launch (start us, length us, event | category | flops | bytes accessed | tf_op | source)
XLA Modules:
  0.0 52.5 jit_solution(16961552704777629760)
XLA Ops:
  0.0 50.6 %attend.1 = bf16[64,4096]{1,0:T(8,128)(2,1)} custom-call(bf16[512,512]{1,0:T(8,128)(2,1)} %q_hbm.1, bf16[4,128,128]{2,1,0:T(8,128)(2,1)} %bitcast.2, bf16[512,128]{1,0:T(8,128)(2,1)} %v_hbm.1, s32[1,32]{1,0:T(1,128)} %bitcast.3), custom_call_target="tpu_custom_call" | custom-call | flops 4294967296 | bytes 2097152 | tf_op jit(solution)/shard_map/attend/pallas_call | solution.py:366
  50.6 1.9 %copy.6 = bf16[64,4096]{1,0:T(8,128)(2,1)} copy(bf16[64,4096]{1,0:T(8,128)(2,1)} %attend.1) | data formatting | bytes 1048576

commit v14 on v10

--- a/solution.py
+++ b/solution.py
@@ -135,7 +135,9 @@
             move(d, d, j, to, lane).wait_send()
 
     for j in range(PIECES):
-        send(0, FAR, j, up)
+        @pl.when(z != 0)
+        def _():
+            send(0, FAR, j, up)
 
         send(0, 1, j, after)
 
@@ -229,9 +231,9 @@
 
     far_steps = 4 * PIECES
     lag = jnp.where(z < 2, LAG_WRAP, LAG)
-    work_from = lag + 1
-
-    @pl.loop(0, 3 * PIECES + 1 + LAG_WRAP)
+    work_from = lag + jnp.where(z == 0, PIECES - 1, 1)
+
+    @pl.loop(0, 4 * PIECES - 1 + LAG_WRAP)
     def _(t):
         j = lax.rem(t, PIECES)
         d = FAR - t // PIECES
@@ -248,10 +250,9 @@
             def _():
                 send(5, 4, j, before, 0)
 
-        @pl.when((z == 0) & (t == work_from))
-        def _():
-            for k in range(PIECES):
-                arrived(FAR, k)
+        @pl.when((z == 0) & (t >= PIECES) & (t < 2 * PIECES))
+        def _():
+            send(0, FAR, j, up)
 
         u = t - lag
         near = u // PIECES + 1
@@ -271,12 +272,18 @@
         def _():
             p = w // PIECES + 1
             i = 2 * lax.rem(w, 2)
-            chunk = jnp.where(lax.rem(w, PIECES) < 2, FAR + 1 - p, p)
+            early = lax.rem(w, PIECES) < 2
+            chunk = jnp.where(z == 0, jnp.where(early, p, FAR - p), jnp.where(early, FAR + 1 - p, p))
             update((i, i + 1), [(chunk, every)])
+
+    @pl.when(z == 0)
+    def _():
+        for j in every:
+            arrived(FAR, j)
 
     @pl.loop(0, PIECES // 2)
     def _(i):
-        update((2 * i, 2 * i + 1), [(5, every)])
+        update((2 * i, 2 * i + 1), [(jnp.where(z == 0, FAR, 5), every)])
 
     for j in every[:half]:
         arrived(4, j)

time: 52.6 us -> 54.5 us (1.036)
  Pallas kernels: 50.6 us -> 52.5 us
    pallas_call x1, Pallas kernels: 50.6 us -> 52.5 us  [body(): pl.pallas_call(functools.partial(kernel, n_seq, n_head), out_shape=jax.Sh...]
where the time goes in v14:
time: 54.5 us; the launch traced here: 54.3 us
  Pallas kernels  52.5 us (96%)
  local copies, waits for them, and re-layouts  1.87 us (3%)
    pallas_call x1, Pallas kernels, body(): pl.pallas_call(functools.partial(kernel, n_seq, n_head), out_shape=jax.Sh...  52.5 us
    unnamed x1, local copies, waits for them, and re-layouts  1.87 us

profile of v14, /device:TPU:49, one launch (start us, length us, event | category | flops | bytes accessed | tf_op | source)
XLA Modules:
  0.0 54.3 jit_solution(151060721773192425)
XLA Ops:
  0.0 52.5 %attend.1 = bf16[64,4096]{1,0:T(8,128)(2,1)} custom-call(bf16[512,512]{1,0:T(8,128)(2,1)} %q_hbm.1, bf16[512,128]{1,0:T(8,128)(2,1)} %k_hbm.1, bf16[512,128]{1,0:T(8,128)(2,1)} %v_hbm.1, s32[1,32]{1,0:T(1,128)} %bitcast.1), custom_call_target="tpu_custom_call" | custom-call | flops 4294967296 | bytes 2097152 | tf_op jit(solution)/shard_map/attend/pallas_call | solution.py:375
  52.5 1.9 %copy.6 = bf16[64,4096]{1,0:T(8,128)(2,1)} copy(bf16[64,4096]{1,0:T(8,128)(2,1)} %attend.1) | data formatting | bytes 1048576

commit v15 on v10

--- a/solution.py
+++ b/solution.py
@@ -267,7 +267,15 @@
 
         w = t - work_from
 
-        @pl.when((w >= 0) & (w < 3 * PIECES))
+        @pl.when(w == 0)
+        def _():
+            update((0, 1), [(FAR, every[1:])])
+
+        @pl.when(w == 1)
+        def _():
+            update((2, 3), [(FAR, every[3:])])
+
+        @pl.when((w >= 2) & (w < 3 * PIECES))
         def _():
             p = w // PIECES + 1
             i = 2 * lax.rem(w, 2)

time: 52.6 us -> 52.7 us (level)
  no operation moved by 1% of the time
where the time goes in v15:
time: 52.7 us; the launch traced here: 52.5 us
  Pallas kernels  50.6 us (96%)
  local copies, waits for them, and re-layouts  1.87 us (4%)
    pallas_call x1, Pallas kernels, body(): pl.pallas_call(functools.partial(kernel, n_seq, n_head), out_shape=jax.Sh...  50.6 us
    unnamed x1, local copies, waits for them, and re-layouts  1.87 us

profile of v15, /device:TPU:49, one launch (start us, length us, event | category | flops | bytes accessed | tf_op | source)
XLA Modules:
  0.0 52.5 jit_solution(6822554615369780653)
XLA Ops:
  0.0 50.6 %attend.1 = bf16[64,4096]{1,0:T(8,128)(2,1)} custom-call(bf16[512,512]{1,0:T(8,128)(2,1)} %q_hbm.1, bf16[512,128]{1,0:T(8,128)(2,1)} %k_hbm.1, bf16[512,128]{1,0:T(8,128)(2,1)} %v_hbm.1, s32[1,32]{1,0:T(1,128)} %bitcast.1), custom_call_target="tpu_custom_call" | custom-call | flops 4294967296 | bytes 2097152 | tf_op jit(solution)/shard_map/attend/pallas_call | solution.py:376
  50.6 1.9 %copy.6 = bf16[64,4096]{1,0:T(8,128)(2,1)} copy(bf16[64,4096]{1,0:T(8,128)(2,1)} %attend.1) | data formatting | bytes 1048576
